TPU v7x, 128 devices: a whole 4x4x4 slice. The times are simulated.
128 devices in a mesh: lon: 32 (over z_hi, x, y), lat: 4 (over z_lo, core).
Axes of the slice: x: 4, y: 4, z: 4 (z_hi: 2, z_lo: 2; z = z_hi * 2 + z_lo), core: 2. Of those that a mesh axis runs over, the one named last changes fastest.
Arguments:
- latents: bfloat16 [2, 144, 768, 512], P(None, 'lat', 'lon'), may hold values from -6 to 6
- region_ids: int32 [2, 144, 768], replicated, may hold values from 0 to 3
- attend_one: bfloat16 [3, 512, 512], replicated, may hold values from -1.2 to 1.2
- project_one: bfloat16 [512, 512], replicated, may hold values from -0.25 to 0.25
- expand_one: bfloat16 [512, 2048], replicated, may hold values from -0.25 to 0.25
- reduce_one: bfloat16 [2048, 512], replicated, may hold values from -0.125 to 0.125
- merge_weight: bfloat16 [2048, 1024], P(('lon', 'lat')), may hold values from -0.125 to 0.125
- attend_two: bfloat16 [3, 1024, 1024], P(None, 'lon', 'lat'), may hold values from -1.2 to 1.2
- project_two: bfloat16 [1024, 1024], P('lat', 'lon'), may hold values from -0.1875 to 0.1875
- expand_two: bfloat16 [1024, 4096], P('lon', 'lat'), may hold values from -0.1875 to 0.1875
- reduce_two: bfloat16 [4096, 1024], P('lat', 'lon'), may hold values from -0.09375 to 0.09375
Outputs:
- encoded: bfloat16 [2, 72, 384, 1024], P(None, None, 'lon', 'lat')
All inputs are finite; a program needn't handle non-finite values.
Results may differ from a plain program's by a relative error of at most 0.018.
Values may be sent and summed in bfloat16 or wider, within the bound.
A program may use at most 192 MiB of HBM per device.

v0:
```python
import jax
import jax.numpy as jnp
from jax import lax
from jax.sharding import PartitionSpec as P

H1 = 8
H2 = 16
WLAT = 6
WLON = 12


EPSILON = 1e-05
MASKED = -1e30


def passed_along(value, axis, steps):
    count = lax.axis_size(axis)
    pairs = [(source, (source + steps) % count) for source in range(count)]
    return lax.ppermute(value, axis, pairs)


def layer_norm(values):
    values = values.astype(jnp.float32)
    centered = values - jnp.mean(values, axis=-1, keepdims=True)
    variance = jnp.mean(centered * centered, axis=-1, keepdims=True)
    return centered / jnp.sqrt(variance + EPSILON)


def to_windows(source, win_lat, win_lon):
    levels, height, extent = (source.shape[0], source.shape[1], source.shape[2])
    trailing = source.shape[3:]
    shaped = source.reshape(
        (levels, height // win_lat, win_lat, extent // win_lon, win_lon) + trailing
    )
    order = (1, 3, 0, 2, 4) + tuple(range(5, 5 + len(trailing)))
    return shaped.transpose(order).reshape(
        (height // win_lat * (extent // win_lon), levels * win_lat * win_lon) + trailing
    )


def from_windows(windows, levels, height, extent, win_lat, win_lon):
    trailing = windows.shape[2:]
    shaped = windows.reshape(
        (height // win_lat, extent // win_lon, levels, win_lat, win_lon) + trailing
    )
    order = (2, 0, 3, 1, 4) + tuple(range(5, 5 + len(trailing)))
    return shaped.transpose(order).reshape((levels, height, extent) + trailing)


def window_attention(packed, region, head_count):
    window_count = packed.shape[0]
    window_len = packed.shape[1]
    channels = packed.shape[3]
    head_size = channels // head_count
    parted = packed.reshape(window_count, window_len, 3, head_count, head_size)
    scores = jnp.einsum(
        "wqhd,wkhd->whqk", parted[:, :, 0], parted[:, :, 1], preferred_element_type=jnp.float32
    ) * head_size ** (-0.5)
    if region is not None:
        matching = region[:, :, None] == region[:, None, :]
        scores = jnp.where(matching[:, None], scores, MASKED)
    highest = jnp.max(scores, axis=-1, keepdims=True)
    lifted = jnp.exp(scores - highest)
    chances = (lifted / jnp.sum(lifted, axis=-1, keepdims=True)).astype(jnp.bfloat16)
    blended = jnp.einsum(
        "whqk,wkhd->wqhd", chances, parted[:, :, 2], preferred_element_type=jnp.float32
    )
    return blended.astype(jnp.bfloat16).reshape(window_count, window_len, channels)


def tile_attention(source, region, attend, head_count):
    levels, height, extent, channels = source.shape
    normed = layer_norm(source).astype(jnp.bfloat16)
    packed = jnp.einsum(
        "abci,kio->abcko", normed, attend, preferred_element_type=jnp.float32
    ).astype(jnp.bfloat16)
    blended = window_attention(
        to_windows(packed, WLAT, WLON), to_windows(region, WLAT, WLON), head_count
    )
    return from_windows(blended, levels, height, extent, WLAT, WLON)


def finish_local(source, blended, project, expand, shrink):
    channels = source.shape[-1]
    flattened = source.reshape(-1, channels)
    hidden = (
        flattened.astype(jnp.float32)
        + jnp.dot(blended.reshape(-1, channels), project, preferred_element_type=jnp.float32)
    ).astype(jnp.bfloat16)
    activated = jax.nn.gelu(
        jnp.dot(layer_norm(hidden).astype(jnp.bfloat16), expand, preferred_element_type=jnp.float32)
    ).astype(jnp.bfloat16)
    result = (
        hidden.astype(jnp.float32) + jnp.dot(activated, shrink, preferred_element_type=jnp.float32)
    ).astype(jnp.bfloat16)
    return result.reshape(source.shape)


def triple_product(normed, weight_shard):
    whole_weight = lax.all_gather(weight_shard, "lon", axis=1, tiled=True)
    return jnp.einsum("ti,kio->tko", normed, whole_weight, preferred_element_type=jnp.float32)


def output_map(blended, weight_shard):
    return jnp.dot(
        blended,
        lax.all_gather(weight_shard, "lon", axis=1, tiled=True),
        preferred_element_type=jnp.float32,
    )


def expand_product(normed, weight_shard):
    whole_weight = lax.all_gather(weight_shard, "lon", axis=0, tiled=True)
    return jnp.dot(normed, whole_weight, preferred_element_type=jnp.float32)


def reduce_map(activated, weight_shard):
    return jnp.dot(
        activated,
        lax.all_gather(weight_shard, "lon", axis=1, tiled=True),
        preferred_element_type=jnp.float32,
    )


def second_attention(source, attend_shard):
    levels, height, extent, channels = source.shape
    slice_width = attend_shard.shape[2]
    head_count = H2 * slice_width // channels
    normed = layer_norm(source).astype(jnp.bfloat16).reshape(-1, channels)
    packed = (
        triple_product(normed, attend_shard)
        .astype(jnp.bfloat16)
        .reshape(levels, height, extent, 3, slice_width)
    )
    blended = window_attention(to_windows(packed, WLAT, WLON), None, head_count)
    return from_windows(blended, levels, height, extent, WLAT, WLON).reshape(-1, slice_width)


def body(
    latents,
    region_ids,
    attend_one,
    project_one,
    expand_one,
    reduce_one,
    merge_weight,
    attend_two,
    project_two,
    expand_two,
    reduce_two,
):
    levels, tile_rows, tile_cols, width_one = latents.shape
    half_lat = WLAT // 2
    half_lon = WLON // 2
    lat_index = lax.axis_index("lat")
    lon_index = lax.axis_index("lon")
    from_right = passed_along(latents[:, :, :half_lon], "lon", -1)
    widened = jnp.concatenate([latents[:, :, half_lon:], from_right], axis=2)
    from_above = passed_along(widened[:, :half_lat], "lat", -1)
    shifted = jnp.concatenate([widened[:, half_lat:], from_above], axis=1)
    rolled_ids = jnp.roll(region_ids, (-half_lat, -half_lon), axis=(1, 2))
    region_tile = lax.dynamic_slice(
        rolled_ids,
        (0, lat_index * tile_rows, lon_index * tile_cols),
        (levels, tile_rows, tile_cols),
    )
    blended = tile_attention(shifted, region_tile, attend_one, H1)
    finished = finish_local(shifted, blended, project_one, expand_one, reduce_one)
    from_below = passed_along(finished[:, tile_rows - half_lat :], "lat", 1)
    restored = jnp.concatenate([from_below, finished[:, : tile_rows - half_lat]], axis=1)
    from_left = passed_along(restored[:, :, tile_cols - half_lon :], "lon", 1)
    section_one = jnp.concatenate([from_left, restored[:, :, : tile_cols - half_lon]], axis=2)
    quartets = (
        section_one.reshape(levels, tile_rows // 2, 2, tile_cols // 2, 2, width_one)
        .transpose(0, 1, 3, 4, 2, 5)
        .reshape(-1, 4 * width_one)
    )
    merge_input = layer_norm(quartets).astype(jnp.bfloat16)
    width_two = merge_weight.shape[1]
    merge_whole = lax.all_gather(merge_weight, ("lon", "lat"), axis=0, tiled=True)
    merged = jnp.dot(merge_input, merge_whole, preferred_element_type=jnp.float32)
    merged = merged.astype(jnp.bfloat16).reshape(levels, tile_rows // 2, tile_cols // 2, width_two)
    attend_all, project_all, expand_all, reduce_all = (
        lax.all_gather(attend_two, "lat", axis=2, tiled=True),
        lax.all_gather(project_two, "lat", axis=0, tiled=True),
        lax.all_gather(expand_two, "lat", axis=1, tiled=True),
        lax.all_gather(reduce_two, "lat", axis=0, tiled=True),
    )
    blended = second_attention(merged, attend_all)
    flattened = merged.reshape(-1, width_two)
    hidden = (flattened.astype(jnp.float32) + output_map(blended, project_all)).astype(jnp.bfloat16)
    activated = jax.nn.gelu(
        expand_product(layer_norm(hidden).astype(jnp.bfloat16), expand_all)
    ).astype(jnp.bfloat16)
    result = (hidden.astype(jnp.float32) + reduce_map(activated, reduce_all)).astype(jnp.bfloat16)
    result = result.reshape(merged.shape)
    encoded = lax.all_to_all(result, "lat", split_axis=3, concat_axis=1, tiled=True)
    return encoded


def solution(mesh):
    return jax.shard_map(
        body,
        mesh=mesh,
        in_specs=(
            P(None, "lat", "lon", None),
            P(),
            P(),
            P(),
            P(),
            P(),
            P(("lon", "lat"), None),
            P(None, "lon", "lat"),
            P("lat", "lon"),
            P("lon", "lat"),
            P("lat", "lon"),
        ),
        out_specs=P(None, None, "lon", "lat"),
        check_vma=False,
    )
```

profile of v0, /device:TPU:1, one launch (start us, length us, event | category | flops | bytes accessed | tf_op | source)
XLA Modules:
  0.0 688.4 jit_solution(15742369399980745263)
XLA Ops:
  7.3 8.9 %all_gather.28 = bf16[3,32,1024]{2,1,0:T(8,128)(2,1)} all-gather(bf16[3,32,256]{2,1,0:T(8,128)(2,1)} %param.18), channel_id=1, replica_groups=mesh['lon'=32,'lat'=4] {'lat'}, dimensions={2}, use_global_device_ids=true | all-gather | bytes 245760 | tf_op jit(solution)/shard_map/all_gather | solution.py:184
  16.3 6.0 all_gather.30
  22.4 7.7 %all_gather.32 = bf16[32,4096]{1,0:T(8,128)(2,1)} all-gather(bf16[32,1024]{1,0:T(8,128)(2,1)} %param.20), channel_id=1, replica_groups=mesh['lon'=32,'lat'=4] {'lat'}, dimensions={1}, use_global_device_ids=true | all-gather | bytes 327680 | tf_op jit(solution)/shard_map/all_gather | solution.py:186
  31.4 7.8 %collective-permute-start = (bf16[2,36,6,512]{3,1,2,0:T(8,128)(2,1)S(1)}, bf16[2,36,6,512]{3,1,2,0:T(8,128)(2,1)}, u32[]{:S(2)}, u32[]{:S(2)}) collective-permute-start(bf16[2,36,6,512]{3,1,2,0:T(8,128)(2,1)S(1)} %copy.153), channel_id=1, source_target_pairs={{0,124},{4,0},{8,4},{12,8},{16,12},{20,16},{24,20},{28,24},{32,28}... | collective-permute-start | bytes 1327112 | tf_op jit(solution)/shard_map/ppermute | solution.py:19
  39.3 6.8 all_gather.34
  46.1 3.6 slice.58
  55.6 4.5 collective-permute-done.1
  61.3 3.6 convolution_convert_fusion
  65.0 13.4 %copy.119 = bf16[2,36,24,3,512]{4,0,3,2,1:T(2,128)(2,1)S(1)} copy(bf16[2,36,24,3,512]{4,2,3,1,0:T(8,128)(2,1)S(1)} %convolution_convert_fusion) | data formatting | bytes 10616832 | tf_op jit(solution)/shard_map/convert_element_type | solution.py:76
  78.4 3.8 copy.120
  82.3 17.2 %reshape_reshape.21 = bf16[12,144,3,8,64]{4,3,0,2,1:T(8,128)(2,1)} reshape(bf16[6,2,2,6,12,3,512]{6,1,0,5,4,3,2:T(2,128)(2,1)} %copy.120) | data formatting | bytes 10616832 | tf_op jit(solution)/shard_map/reshape;reshape | solution.py:55
  99.4 7.9 %fusion.114 = (bf16[12,144,1,8,64]{4,3,0,2,1:T(8,128)(2,1)}, bf16[12,144,1,8,64]{4,3,0,2,1:T(8,128)(2,1)}, bf16[12,144,1,8,64]{4,3,0,2,1:T(8,128)(2,1)}) fusion(bf16[12,144,3,8,64]{4,3,0,2,1:T(8,128)(2,1)} %reshape_reshape.21), kind=kLoop, calls=%fused_computation.134 | loop fusion | bytes 10616832 | tf_op jit(solution)/shard_map/slice | solution.py:66
  107.3 6.5 copy.155
  113.8 6.5 copy.156
  120.4 6.6 copy.154
  126.9 13.3 %fusion.116 = (f32[12,8,144]{2,1,0:T(8,128)S(1)}, f32[12,8,144,144]{2,3,1,0:T(8,128)}) fusion(pred[12,144,144]{1,2,0:T(8,128)(4,1)S(1)} %broadcast_compare_fusion, bf16[12,144,1,8,64]{1,4,3,0,2:T(8,128)(2,1)} %copy.156, bf16[12,144,1,8,64]{1,4,3,0,2:T(8,128)(2,1)} %copy.155), kind=kOutput, calls=%fused_computation.136 | convolution fusion | flops 262766736 | bytes 11805696 | tf_op jit(solution)/shard_map/sub | solution.py:63
  140.2 8.8 %convert_bitcast_fusion.1 = bf16[12,144,8,64]{1,3,2,0:T(8,128)(2,1)} fusion(f32[12,8,144,144]{2,3,1,0:T(8,128)} %get-tuple-element.12, f32[12,8,144]{2,1,0:T(8,128)S(1)} %get-tuple-element.11, bf16[12,144,1,8,64]{1,4,3,0,2:T(8,128)(2,1)} %copy.154), kind=kOutput, calls=%fused_computation.58 | convolution fusion | flops 259670016 | bytes 11556864 | tf_op jit(solution)/shard_map/whqk,wkhd->wqhd/dot_general | solution.py:65
  149.0 6.7 copy.127
  155.8 6.9 %reshape_reshape.22 = bf16[6,2,2,6,12,512]{5,1,0,4,3,2:T(2,128)(2,1)} reshape(bf16[12,144,8,64]{3,2,0,1:T(8,128)(2,1)} %copy.127) | data formatting | bytes 3538944 | tf_op jit(solution)/shard_map/reshape;reshape | solution.py:43
  162.7 3.5 copy.128
  166.2 3.9 reshape_reshape.23
  170.0 3.0 bitcast_add_fusion
  175.2 11.8 %fusion.30 = bf16[1728,512]{1,0:T(8,128)(2,1)} fusion(bf16[2048,512]{1,0:T(8,128)(2,1)S(1)} %copy-done, bf16[512,2048]{1,0:T(8,128)(2,1)} %param.15, f32[1728]{0:T(1024)S(1)} %add_sqrt_fusion.2, f32[1728]{0:T(1024)S(1)} %broadcast_multiply_fusion.2, bf16[1728,512]{1,0:T(8,128)(2,1)} %copy-done.4), kind=kOutput, calls=%fused_computation.39 | convolution fusion | flops 7285800960 | bytes 7747072 | tf_op jit(solution)/shard_map/dot_general | solution.py:94
  193.7 14.9 %collective-permute-done.3 = bf16[2,36,6,512]{3,0,2,1:T(2,128)(2,1)S(1)} collective-permute-done((bf16[2,36,6,512]{3,0,2,1:T(2,128)(2,1)S(1)}, bf16[2,36,6,512]{3,0,2,1:T(2,128)(2,1)S(1)}, u32[]{:S(2)}, u32[]{:S(2)}) %collective-permute-start.3) | collective-permute-done | bytes 442400 | tf_op jit(solution)/shard_map/ppermute | solution.py:19
  217.0 4.5 copy.131
  221.5 6.0 reshape.129
  227.6 5.6 convert_reduce_fusion.3
  233.6 78.1 %all-gather.8.cloned.1.call-done = bf16[3,1024,1024]{2,1,0:T(8,128)(2,1)} async-done(((bf16[3,32,1024]{2,1,0:T(8,128)(2,1)}), bf16[3,1024,1024]{2,1,0:T(8,128)(2,1)}) %all-gather.8.cloned.1.call-update) | async-done | bytes 6291472 | tf_op jit(solution)/shard_map/all_gather | solution.py:100
  311.7 7.3 %convolution_convert_fusion.1 = bf16[432,3,1024]{2,0,1:T(8,128)(2,1)} fusion(bf16[3,1024,1024]{2,1,0:T(8,128)(2,1)} %all-gather.8.cloned.1.call-done, bf16[432,1024]{1,0:T(8,128)(2,1)S(1)} %get-tuple-element.14, f32[432]{0:T(512)S(1)} %add_sqrt_fusion.4, f32[432]{0:T(512)S(1)} %broadcast_multiply_fusion.4), kind=kOutput, calls=%fused_computation.70 | convolution fusion | flops 2721005568 | bytes 9833856 | tf_op jit(solution)/shard_map/ti,kio->tko/dot_general | solution.py:101
  319.0 5.2 reshape_reshape.24
  324.2 4.5 copy.137
  328.7 8.7 %reshape_reshape.25 = bf16[3,144,3,16,64]{4,3,1,2,0:T(8,128)(2,1)} reshape(bf16[3,1,2,6,12,3,1024]{6,4,3,2,5,0,1:T(8,128)(2,1)} %copy.137) | data formatting | bytes 5308416 | tf_op jit(solution)/shard_map/reshape;reshape | solution.py:55
  337.4 5.3 fusion.115
  342.7 3.1 copy.160
  345.8 4.1 copy.161
  349.9 4.1 copy.159
  356.5 6.7 fusion.121
  365.1 3.1 copy.142
  370.3 13.7 %all-gather.10.cloned.1.call-done = bf16[1024,1024]{0,1:T(8,128)(2,1)} async-done(((bf16[1024,32]{0,1:T(8,128)(2,1)}), bf16[1024,1024]{0,1:T(8,128)(2,1)}) %all-gather.10.cloned.1.call-update) | async-done | bytes 2097168 | tf_op jit(solution)/shard_map/all_gather | solution.py:107
  384.0 2.8 convert_reduce_fusion.2
  387.2 102.6 %all-gather.12.cloned.1.call-done = bf16[1024,4096]{1,0:T(8,128)(2,1)} async-done(((bf16[32,4096]{1,0:T(8,128)(2,1)}), bf16[1024,4096]{1,0:T(8,128)(2,1)}) %all-gather.12.cloned.1.call-update) | async-done | bytes 8388624 | tf_op jit(solution)/shard_map/all_gather | solution.py:113
  489.7 105.7 %all-gather.14.cloned.1.call-done = bf16[4096,1024]{0,1:T(8,128)(2,1)} async-done(((bf16[4096,32]{0,1:T(8,128)(2,1)}), bf16[4096,1024]{0,1:T(8,128)(2,1)}) %all-gather.14.cloned.1.call-update) | async-done | bytes 8388624 | tf_op jit(solution)/shard_map/all_gather | solution.py:120
  595.5 13.7 %fusion.56 = bf16[432,1024]{1,0:T(8,128)(2,1)S(1)} fusion(bf16[432,1024]{1,0:T(8,128)(2,1)S(1)} %get-tuple-element.18, bf16[4096,1024]{0,1:T(8,128)(2,1)} %all-gather.14.cloned.1.call-done, bf16[1024,4096]{1,0:T(8,128)(2,1)} %all-gather.12.cloned.1.call-done, f32[432]{0:T(512)S(1)} %add_sqrt_fusion.3, f32[432]{0:T(512)S(1)} %broadcast_multiply_fusion.3), kind=kOutput, calls=%fused_computation.76 | convolution fusion | flops 7266779136 | bytes 18550144 | tf_op jit(solution)/shard_map/dot_general | solution.py:118
  609.4 10.7 %copy.144 = bf16[2,18,12,1024]{1,0,2,3:T(2,128)(2,1)} copy(bf16[2,18,12,1024]{3,2,1,0:T(8,128)(2,1)S(1)} %reshape.127) | data formatting | bytes 1769472 | tf_op jit(solution)/shard_map/reshape | solution.py:196
  620.1 12.8 %reshape.135 = bf16[4,2,55296]{2,1,0:T(2,128)(2,1)S(1)} reshape(bf16[1024,12,2,18]{3,2,1,0:T(2,128)(2,1)} %bitcast.111) | data formatting | bytes 1769472
  632.8 15.4 %all_to_all.18 = bf16[4,2,55296]{2,1,0:T(2,128)(2,1)S(1)} all-to-all(bf16[4,2,55296]{2,1,0:T(2,128)(2,1)S(1)} %reshape.135), channel_id=1, replica_groups=mesh['lon'=32,'lat'=4] {'lat'}, dimensions={0} | all-to-all | bytes 1769472 | tf_op jit(solution)/shard_map/all_to_all | solution.py:197
  648.2 16.8 %reshape.136 = bf16[1024,12,2,18]{3,2,1,0:T(2,128)(2,1)} reshape(bf16[4,2,55296]{2,1,0:T(2,128)(2,1)S(1)} %all_to_all.18) | data formatting | bytes 1769472
  665.0 14.8 %copy.152 = bf16[2,18,12,4,256]{4,3,0,2,1:T(4,128)(2,1)S(1)} copy(bf16[2,18,12,4,256]{1,0,2,4,3:T(2,128)(2,1)} %bitcast.112) | data formatting | bytes 1769472 | tf_op jit(solution)/shard_map/all_to_all | solution.py:197
  (92 shorter events, 35.6 us)
Async XLA Ops:
  6.5 168.7 %copy-start = (bf16[2048,512]{1,0:T(8,128)(2,1)S(1)}, bf16[2048,512]{1,0:T(8,128)(2,1)}, u32[]{:S(2)}) copy-start(bf16[2048,512]{1,0:T(8,128)(2,1)} %param.16) | copy-start | bytes 6291460
  6.5 32.8 %copy-start.8 = (bf16[1024,32]{0,1:T(8,128)(2,1)S(1)}, bf16[1024,32]{0,1:T(8,128)(2,1)}, u32[]{:S(2)}) copy-start(bf16[1024,32]{0,1:T(8,128)(2,1)} %param.21) | copy-start | bytes 196612
  6.5 221.1 %all-gather.6.cloned.1.call-start = ((), (), s32[]{:S(2)}) async-start(), calls=%async_computation.1 | async-start | bytes 4227072 | tf_op jit(solution)/shard_map/all_gather | solution.py:180
  7.3 304.5 %all-gather.8.cloned.1.call-start = ((), (), s32[]{:S(2)}) async-start(), calls=%async_computation.2 | async-start | bytes 6488064 | tf_op jit(solution)/shard_map/all_gather | solution.py:100
  16.3 367.7 %all-gather.10.cloned.1.call-start = ((), (), s32[]{:S(2)}) async-start(), calls=%async_computation.3 | async-start | bytes 2162688 | tf_op jit(solution)/shard_map/all_gather | solution.py:107
  22.3 467.4 %all-gather.12.cloned.1.call-start = ((), (), s32[]{:S(2)}) async-start(), calls=%async_computation.4 | async-start | bytes 8650752 | tf_op jit(solution)/shard_map/all_gather | solution.py:113
  30.1 565.3 %all-gather.14.cloned.1.call-start = ((), (), s32[]{:S(2)}) async-start(), calls=%async_computation.5 | async-start | bytes 8650752 | tf_op jit(solution)/shard_map/all_gather | solution.py:120
  31.4 21.3 %collective-permute-start = (bf16[2,36,6,512]{3,1,2,0:T(8,128)(2,1)S(1)}, bf16[2,36,6,512]{3,1,2,0:T(8,128)(2,1)}, u32[]{:S(2)}, u32[]{:S(2)}) collective-permute-start(bf16[2,36,6,512]{3,1,2,0:T(8,128)(2,1)S(1)} %copy.153), channel_id=1, source_target_pairs={{0,124},{4,0},{8,4},{12,8},{16,12},{20,16},{24,20},{28,24},{32,28}... | collective-permute-start | bytes 1327112 | tf_op jit(solution)/shard_map/ppermute | solution.py:19
  52.4 2.9 copy-start.2
  55.1 6.3 copy-start.9
  55.1 5.1 collective-permute-start.1
  55.6 9.4 %copy-start.3 = (bf16[2,33,24,512]{3,2,1,0:T(8,128)(2,1)}, bf16[2,33,24,512]{3,2,1,0:T(8,128)(2,1)S(1)}, u32[]{:S(2)}) copy-start(bf16[2,33,24,512]{3,2,1,0:T(8,128)(2,1)S(1)} %fusion.68) | copy-start | bytes 4866052
  162.7 7.4 %copy-start.10 = (bf16[512,512]{1,0:T(8,128)(2,1)S(1)}, bf16[512,512]{1,0:T(8,128)(2,1)}, u32[]{:S(2)}) copy-start(bf16[512,512]{1,0:T(8,128)(2,1)} %param.14) | copy-start | bytes 1572868
  173.1 1.2 copy-start.4
  188.1 2.3 collective-permute-start.2
  192.5 16.1 %collective-permute-start.3 = (bf16[2,36,6,512]{3,0,2,1:T(2,128)(2,1)S(1)}, bf16[2,36,6,512]{3,0,2,1:T(2,128)(2,1)S(1)}, u32[]{:S(2)}, u32[]{:S(2)}) collective-permute-start(bf16[2,36,6,512]{3,0,2,1:T(2,128)(2,1)S(1)} %slice.85), channel_id=1, source_target_pairs={{0,4},{4,8},{8,12},{12,16},{16,20},{20,24},{24,28},{28,32},{32,36}... | collective-permute-start | bytes 1327112 | tf_op jit(solution)/shard_map/ppermute | solution.py:19
  233.2 85.8 %copy-start.6 = (bf16[432,1024]{1,0:T(8,128)(2,1)}, bf16[432,1024]{1,0:T(8,128)(2,1)S(1)}, u32[]{:S(2)}) copy-start(bf16[432,1024]{1,0:T(8,128)(2,1)S(1)} %get-tuple-element.14) | copy-start | bytes 2654212
  356.5 6.7 copy-start.5
  369.9 14.0 %copy-start.7 = (bf16[432,1024]{1,0:T(8,128)(2,1)S(1)}, bf16[432,1024]{1,0:T(8,128)(2,1)}, u32[]{:S(2)}) copy-start(bf16[432,1024]{1,0:T(8,128)(2,1)} %copy-done.6) | copy-start | bytes 2654212
  665.0 16.6 %copy-start.1 = (bf16[2048,512]{1,0:T(8,128)(2,1)S(1)}, bf16[2048,512]{1,0:T(8,128)(2,1)}, u32[]{:S(2)}) copy-start(bf16[2048,512]{1,0:T(8,128)(2,1)} %param.16) | copy-start | bytes 6291460
Sparse Core Ops, SparseCore 0:
  9.1 209.7 all-gather.5
  221.9 89.7 all-gather.7
  314.8 69.1 all-gather.9
  386.9 102.7 all-gather.11
  492.7 102.7 all-gather.13
where the time goes:
time: 696 us; the launch traced here: 688 us
  waiting for transfers between devices  321 us (46%)
  local copies, waits for them, and re-layouts  206 us (30%)
  matrix products  74.3 us (11%)
  blocking collectives  44.8 us (6%)
  other arithmetic  19.6 us (3%)
  between operations  13.8 us (2%)
  starting transfers between devices  8.55 us (1%)
    all_gather x1, waiting for transfers between devices, reduce_map(): lax.all_gather(weight_shard, 'lon', axis=1, tiled=True)  106 us
    all_gather x1, waiting for transfers between devices, expand_product(): whole_weight = lax.all_gather(weight_shard, 'lon', axis=0, tiled=True)  103 us
    all_gather x1, waiting for transfers between devices, triple_product(): whole_weight = lax.all_gather(weight_shard, 'lon', axis=1, tiled=True)  78.1 us
    unnamed x33, local copies, waits for them, and re-layouts  61.8 us
    another operation x2, local copies, waits for them, and re-layouts, window_attention(): parted = packed.reshape(window_count, window_len, 3, head_count, head_size)  25.9 us
    ppermute x4, waiting for transfers between devices, passed_along(): return lax.ppermute(value, axis, pairs)  20.1 us
    all_to_all x3, local copies, waits for them, and re-layouts, body(): lax.all_to_all(result, 'lat', split_axis=3, concat_axis=1, tiled=True)  16.6 us
    all_to_all x1, blocking collectives, body(): lax.all_to_all(result, 'lat', split_axis=3, concat_axis=1, tiled=True)  15.4 us
  transfers between devices with their start and end apart: 9, of which 7 were waited for; matrix products, arithmetic and copies ran while one was open for 33% of the time, Pallas kernels for 0%

commit v1 on v0

v1 whole, which is shorter than its diff:
```python
import jax
import jax.numpy as jnp
import numpy as np
from jax import lax
from jax.experimental import pallas as pl
from jax.experimental.pallas import tpu as pltpu
from jax.sharding import PartitionSpec as P

MESH = pl.DeviceIdType.MESH
BF = jnp.bfloat16
F32 = jnp.float32
EPSILON = 1e-05
MASKED = -1e30
ORDERS = (("x", "y", "z"), ("y", "z", "x"), ("z", "x", "y"))
WIDTHS = (1280, 1280, 1024)
SUB = (0, -1, 1, 2)


def gather_plan(bufs, send, recv, sibs, sibr):
    lon = lax.axis_index("lon")
    lat = lax.axis_index("lat")
    me = {"x": (lon // 4) % 4, "y": lon % 4, "z": (lon // 16) * 2 + lat // 2}
    core = lat % 2

    def device(pos, c):
        return ((pos["z"] // 2) * 16 + pos["x"] * 4 + pos["y"], (pos["z"] % 2) * 2 + c)

    def shifted(axis, by):
        pos = dict(me)
        pos[axis] = (me[axis] + by + 4) % 4
        return pos

    def part(s, fix, half):
        at = [slice(None) if fix[a] is None else fix[a] for a in ("z", "x", "y")]
        rows = slice(None) if half is None else pl.ds(16 * half, 16)
        return bufs[s].at[core, at[0], at[1], at[2], rows]

    def copy(s, n, fix, axis, by, half=None):
        ref = part(s, fix, half)
        return pltpu.make_async_remote_copy(
            src_ref=ref, dst_ref=ref, send_sem=send.at[s, n], recv_sem=recv.at[s, n],
            device_id=device(shifted(axis, by), core), device_id_type=MESH,
        )

    def sibling(s, k, j):
        ref = part(s, group(s, 3, SUB[k], SUB[j]), None)
        return pltpu.make_async_remote_copy(
            src_ref=ref, dst_ref=ref, send_sem=sibs.at[s, 4 * j + k], recv_sem=sibr.at[s, 4 * j + k],
            device_id=device(me, 1 - core), device_id_type=MESH,
        )

    def group(s, stage, second=0, third=0):
        axes = ORDERS[s]
        fix = dict(me)
        fix[axes[0]] = None
        fix[axes[1]] = (me[axes[1]] + second + 4) % 4
        fix[axes[2]] = (me[axes[2]] + third + 4) % 4
        return fix

    def own(s, by):
        fix = dict(me)
        axis = ORDERS[s][0]
        fix[axis] = (me[axis] + by + 4) % 4
        return fix

    def first(s):
        a = ORDERS[s][0]
        return copy(s, 0, own(s, 0), a, 1), copy(s, 1, own(s, 0), a, -1)

    def first_on(s):
        a = ORDERS[s][0]
        return copy(s, 2, own(s, -1), a, 1, 0), copy(s, 3, own(s, 1), a, -1, 1)

    def second(s):
        a = ORDERS[s][1]
        return copy(s, 4, group(s, 2), a, 1), copy(s, 5, group(s, 2), a, -1)

    def second_on(s):
        a = ORDERS[s][1]
        return copy(s, 6, group(s, 2, -1), a, 1, 0), copy(s, 7, group(s, 2, 1), a, -1, 1)

    def third(s, k):
        a = ORDERS[s][2]
        fix = group(s, 3, SUB[k])
        return copy(s, 8 + 4 * k, fix, a, 1), copy(s, 9 + 4 * k, fix, a, -1)

    def third_on(s, k):
        a = ORDERS[s][2]
        return (
            copy(s, 10 + 4 * k, group(s, 3, SUB[k], -1), a, 1, 0),
            copy(s, 11 + 4 * k, group(s, 3, SUB[k], 1), a, -1, 1),
        )

    def go(copies):
        for c in copies:
            c.start()

    def got(copies):
        for c in copies:
            c.wait_recv()

    streams = range(3)

    def e0():
        for s in streams:
            go(first(s))

    def e1():
        for s in streams:
            got(first(s))
            go(first_on(s))

    def e2():
        for s in streams:
            got(first_on(s))
            go(second(s))
            go(third(s, 0))
        for s in streams:
            sibling(s, 0, 0).start()

    def e3():
        for s in streams:
            got(second(s))
            go(second_on(s))
            go(third(s, 1))
            go(third(s, 2))
        for s in streams:
            sibling(s, 1, 0).start()
            sibling(s, 2, 0).start()
        for s in streams:
            got(third(s, 0))
            go(third_on(s, 0))
            sibling(s, 0, 1).start()
            sibling(s, 0, 2).start()

    def e4():
        for s in streams:
            got(second_on(s))
            go(third(s, 3))
            sibling(s, 3, 0).start()
        for k in (1, 2):
            for s in streams:
                got(third(s, k))
                go(third_on(s, k))
                sibling(s, k, 1).start()
                sibling(s, k, 2).start()

    def e5():
        for s in streams:
            got(third_on(s, 0))
            sibling(s, 0, 3).start()
        for s in streams:
            got(third(s, 3))
            go(third_on(s, 3))
            sibling(s, 3, 1).start()
            sibling(s, 3, 2).start()

    def e6():
        for k in (1, 2):
            for s in streams:
                got(third_on(s, k))
                sibling(s, k, 3).start()

    def e7():
        for s in streams:
            got(third_on(s, 3))
            sibling(s, 3, 3).start()

    def arrived(s):
        for j in range(4):
            for k in range(4):
                sibling(s, k, j).wait_recv()

    def drain():
        for s in streams:
            for c in first(s) + first_on(s) + second(s) + second_on(s):
                c.wait_send()
            for k in range(4):
                for c in third(s, k) + third_on(s, k):
                    c.wait_send()
                for j in range(4):
                    sibling(s, k, j).wait_send()

    partners = [device(shifted(a, d), core) for a in "xyz" for d in (1, -1)] + [device(me, 1 - core)]
    return me, core, (e0, e1, e2, e3, e4, e5, e6, e7), arrived, drain, partners


def normed(values):
    centered = values - jnp.mean(values, axis=-1, keepdims=True)
    variance = jnp.mean(centered * centered, axis=-1, keepdims=True)
    return centered * lax.rsqrt(variance + EPSILON)


def gelu(v):
    return 0.5 * v * (1.0 + jnp.tanh(0.7978845608028654 * (v + 0.044715 * (v * v * v))))


def mm(a, b):
    return jnp.dot(a, b, preferred_element_type=F32)


def mm_nt(a, b):
    return lax.dot_general(a, b, (((1,), (1,)), ((), ())), preferred_element_type=F32)


def attend_heads(q, k, v, bias):
    lane = lax.broadcasted_iota(jnp.int32, q.shape, 1)
    low_f = (lane < 64).astype(F32)
    low = low_f.astype(BF)
    high = (1.0 - low_f).astype(BF)

    def weights(keys):
        s = mm_nt(q, keys)
        if bias is not None:
            s = s + bias
        return jnp.exp(s - jnp.max(s, axis=-1, keepdims=True)).astype(BF)

    even = mm(weights(k * low), v * low + high)
    odd = mm(weights(k * high), v * high + low)
    is_low = lane < 64
    total = jnp.where(is_low, odd, even)
    return (jnp.where(is_low, even, odd) / pltpu.roll(total, 64, 1)).astype(BF)


def kernel(
    tile, reg_row, reg_col, attend, project, expand, shrink,
    pick_row, pick_col, put, quart_row, quart_col, mix, pad,
    in0, in1, in2,
    out,
    b0, b1, b2, rows, cols, y_rows, y_east, y_west, quart, merged, qkv, blend, hidden, norm2, total, result,
    send, recv, sibs, sibr, loc, halo_s, halo_r, back_s, back_r, fin_s, fin_r,
):
    bufs = (b0, b1, b2)
    me, core, events, arrived, drain, partners = gather_plan(bufs, send, recv, sibs, sibr)
    lon = lax.axis_index("lon")
    lat = lax.axis_index("lat")
    west, east = (lon + 31) % 32, (lon + 1) % 32
    above, below = (lat + 3) % 4, (lat + 1) % 4

    local = [
        pltpu.make_async_copy(src, b.at[core, me["z"], me["x"], me["y"]], loc.at[n])
        for n, (src, b) in enumerate(zip((in0, in1, in2), bufs))
    ]
    local.append(pltpu.make_async_copy(tile, rows.at[pl.ds(0, 36)], loc.at[3]))
    for c in local:
        c.start()
    everyone = partners + [(west, lat), (east, lat), (lon, above), (lon, below), (lon, (lat + 2) % 4)]
    everyone += [(west, above), (east, below)]
    barrier = pltpu.get_barrier_semaphore()
    for d in everyone:
        pl.semaphore_signal(barrier, inc=1, device_id=d, device_id_type=MESH)
    pl.semaphore_wait(barrier, len(everyone))

    def remote(src, dst, ssem, rsem, to):
        return pltpu.make_async_remote_copy(
            src_ref=src, dst_ref=dst, send_sem=ssem, recv_sem=rsem, device_id=to, device_id_type=MESH
        )

    halos = [
        remote(tile.at[:, pl.ds(0, 16)], cols.at[pl.ds(0, 36)], halo_s.at[0], halo_r.at[0], (west, lat)),
        remote(tile.at[pl.ds(0, 3)], rows.at[pl.ds(36, 3)], halo_s.at[1], halo_r.at[1], (lon, above)),
        remote(tile.at[pl.ds(0, 3), pl.ds(0, 16)], cols.at[pl.ds(36, 3)], halo_s.at[2], halo_r.at[2], (west, above)),
    ]
    for c in halos:
        c.start()
    for c in local:
        c.wait()
    events[0]()
    for c in halos:
        c.wait_recv()

    def to_east(a):
        span = pl.ds(6 * a + 3, 6)
        return remote(y_east.at[span], y_west.at[span], back_s.at[a], back_r.at[a], (east, lat))

    edge = [
        remote(y_east.at[pl.ds(33, 3)], y_west.at[pl.ds(33, 3)], back_s.at[5], back_r.at[5], (east, lat)),
        remote(y_east.at[pl.ds(36, 3)], y_west.at[pl.ds(0, 3)], back_s.at[6], back_r.at[6], (east, below)),
        remote(y_rows.at[pl.ds(36, 3)], y_rows.at[pl.ds(0, 3)], back_s.at[7], back_r.at[7], (lon, below)),
    ]

    def pair(t, carry):
        a = lax.rem(t + 5, 6)
        span = pl.ds(6 * a + 3, 6)
        own = rows[span].reshape(288, 512)
        side = cols[span].reshape(96, 512)
        x = mm(pick_row[...], own) + mm(pick_col[...], side)
        n = normed(x).astype(BF)
        q = (mm(n, attend[0]) * 0.125).astype(BF)
        k = mm(n, attend[1]).astype(BF)
        v = mm(n, attend[2]).astype(BF)
        parts = []
        for b in range(2):
            same = reg_col[2 * a + b] == reg_row[2 * a + b]
            bias = jnp.where(same, 0.0, MASKED)
            r = slice(144 * b, 144 * b + 144)
            heads = [
                attend_heads(q[r, 128 * h : 128 * h + 128], k[r, 128 * h : 128 * h + 128], v[r, 128 * h : 128 * h + 128], bias)
                for h in range(4)
            ]
            parts.append(jnp.concatenate(heads, axis=1))
        o = jnp.concatenate(parts, axis=0)

        @pl.when(t == 0)
        def _():
            events[1]()

        hid = (x + mm(o, project[...])).astype(BF)
        hid_f = hid.astype(F32)
        n = normed(hid_f).astype(BF)
        acc = hid_f
        for c in range(4):
            u = gelu(mm(n, expand[:, 512 * c : 512 * c + 512])).astype(BF)
            acc = acc + mm(u, shrink[512 * c : 512 * c + 512, :])
        placed = mm(put[...], acc.astype(BF)).astype(BF)
        y_rows[span] = placed[:288].reshape(6, 48, 512)
        y_east[span] = placed[288:].reshape(6, 16, 512)

        @pl.when(t == 0)
        def _():
            for c in edge:
                c.start()

        @pl.when(t > 0)
        def _():
            to_east(a).start()

        for at, event in ((0, 2), (1, 3), (3, 4), (4, 5), (5, 6)):

            @pl.when(t == at)
            def _(event=event):
                events[event]()

        return carry

    lax.fori_loop(0, 6, pair, 0)
    events[7]()

    for c in edge:
        c.wait_recv()
    for a in range(5):
        to_east(a).wait_recv()

    for w in range(3):
        span = pl.ds(12 * w, 12)
        both = y_rows[span].reshape(6, 2, 48, 512)
        side = y_west[span].reshape(6, 2, 16, 512)
        found = []
        for odd in range(2):
            got = mm(quart_row[...], both[:, odd].reshape(288, 512)) + mm(quart_col[...], side[:, odd].reshape(96, 512))
            found.append(got)
        quads = [found[0][:144], found[1][:144], found[0][144:], found[1][144:]]
        mean = sum(jnp.sum(p, axis=-1, keepdims=True) for p in quads) * (1.0 / 2048.0)
        quads = [p - mean for p in quads]
        variance = sum(jnp.sum(p * p, axis=-1, keepdims=True) for p in quads) * (1.0 / 2048.0)
        scale = lax.rsqrt(variance + EPSILON)
        for p in range(4):
            quart[p, pl.ds(144 * w, 144)] = mm((quads[p] * scale).astype(BF), mix[...]).astype(BF)

    arrived(0)
    for half in range(2):
        acc = jnp.zeros((432, 512), F32)
        for z in range(4):
            for c in range(2):
                ch = slice(128 * ((z % 2) * 2 + c), 128 * ((z % 2) * 2 + c) + 128)
                left = jnp.concatenate([quart[z // 2 * 2, :, ch], quart[z // 2 * 2 + 1, :, ch]], axis=1)
                right = b0[c, z, :, :, pl.ds(16 * half, 16), pl.ds(768, 512)].reshape(256, 512)
                acc = acc + mm(left, right)
        merged[:, pl.ds(512 * half, 512)] = acc.astype(BF)

    norm2[...] = normed(merged[...].astype(F32)).astype(BF)

    def attend_slice(g, carry):
        z_lo, c = g // 2, g % 2
        acc = mm(norm2[:, pl.ds(0, 512)], b0[c, z_lo, :, :, :, pl.ds(0, 768)].reshape(512, 768))
        acc = acc + mm(norm2[:, pl.ds(512, 512)], b0[c, z_lo + 2, :, :, :, pl.ds(0, 768)].reshape(512, 768))
        q = (acc[:, :256] * 0.125).astype(BF)
        qkv[:, pl.ds(0, 256)] = q
        qkv[:, pl.ds(256, 512)] = acc[:, 256:].astype(BF)
        for w in range(3):
            r = pl.ds(144 * w, 144)
            for h in range(2):
                blend[g, r, pl.ds(128 * h, 128)] = attend_heads(
                    qkv[r, pl.ds(128 * h, 128)], qkv[r, pl.ds(256 + 128 * h, 128)], qkv[r, pl.ds(512 + 128 * h, 128)], None
                )
        return carry

    lax.fori_loop(0, 4, attend_slice, 0)

    arrived(1)
    for half in range(2):
        acc = merged[:, pl.ds(512 * half, 512)].astype(F32)
        for g in range(4):
            w_t = b1[g % 2, 2 * half + g // 2, :, :, :, pl.ds(1024, 256)].reshape(512, 256)
            acc = acc + mm_nt(blend[g], w_t)
        hidden[:, pl.ds(512 * half, 512)] = acc.astype(BF)
    total[...] = hidden[...].astype(F32)
    norm2[...] = normed(total[...]).astype(BF)
    arrived(2)

    def feed(g, carry):
        z_lo, c = g // 2, g % 2
        u = mm(norm2[:, pl.ds(0, 512)], b1[c, z_lo, :, :, :, pl.ds(0, 1024)].reshape(512, 1024))
        u = u + mm(norm2[:, pl.ds(512, 512)], b1[c, z_lo + 2, :, :, :, pl.ds(0, 1024)].reshape(512, 1024))
        u = gelu(u).astype(BF)
        for half in range(2):
            h = pl.ds(512 * half, 512)
            total[:, h] += mm_nt(u, b2[c, z_lo + 2 * half].reshape(512, 1024))
        return carry

    lax.fori_loop(0, 4, feed, 0)

    for w in range(3):
        spread = mm(pad[...], total[pl.ds(144 * w, 144)].astype(BF)).astype(BF).reshape(12, 16, 1024)
        for p in range(4):
            for level in range(2):
                result[p, level, pl.ds(6 * w, 6)] = spread[6 * level : 6 * level + 6, :12, 256 * p : 256 * p + 256]

    mine = out.at[:, pl.ds(18 * lat, 18)]
    keep = pltpu.make_async_copy(result.at[lat], mine, loc.at[4])
    last = [remote(result.at[(lat + d) % 4], mine, fin_s.at[d - 1], fin_r.at[d - 1], (lon, (lat + d) % 4)) for d in (1, 2, 3)]
    for c in last:
        c.start()
    keep.start()
    keep.wait()
    for c in last:
        c.wait()
    drain()
    for c in halos + edge + [to_east(a) for a in range(5)]:
        c.wait_send()


def choose(shape, pairs):
    out = np.zeros(shape, np.float32)
    for r, c in pairs:
        out[r, c] = 1.0
    return jnp.asarray(out, BF)


def choices():
    row, col, put_to, qrow, qcol = [], [], [], [], []
    for b in range(2):
        for rho in range(6):
            for hh in range(2):
                for lc in range(12):
                    i = b * 144 + rho * 24 + hh * 12 + lc
                    h = 1 + 2 * b + hh
                    if h < 4:
                        row.append((i, rho * 48 + h * 12 + lc))
                        put_to.append((rho * 48 + (h - 1) * 12 + lc, i))
                    else:
                        col.append((i, rho * 16 + lc))
                        put_to.append((288 + rho * 16 + lc, i))
    for pc in range(2):
        for level in range(2):
            for ii in range(6):
                for j in range(12):
                    i = pc * 144 + level * 72 + ii * 12 + j
                    h, c = divmod(2 * j + pc, 6)
                    if h:
                        qrow.append((i, ii * 48 + (h - 1) * 12 + level * 6 + c))
                    else:
                        qcol.append((i, ii * 16 + level * 6 + c))
    mix = [(blk * 64 + g * 16 + r, g * 128 + blk * 16 + r) for g in range(4) for blk in range(8) for r in range(16)]
    pad = [(g * 16 + j, g * 12 + j) for g in range(12) for j in range(12)]
    return (
        choose((288, 288), row), choose((288, 96), col), choose((384, 288), put_to),
        choose((288, 288), qrow), choose((288, 96), qcol), choose((512, 512), mix), choose((192, 144), pad),
    )


def window_ids(region_ids):
    lat = lax.axis_index("lat")
    lon = lax.axis_index("lon")

    def rows_of(col, width):
        own = lax.dynamic_slice(region_ids, (0, lat * 36, col), (2, 36, width))
        under = lax.dynamic_slice(region_ids, (0, (lat + 1) % 4 * 36, col), (2, 3, width))
        return jnp.concatenate([own[:, 3:], under], axis=1)

    ids = jnp.concatenate([rows_of(lon * 24, 24)[:, :, 6:], rows_of((lon + 1) % 32 * 24, 6)], axis=2)
    ids = ids.reshape(2, 6, 6, 2, 2, 6).transpose(1, 3, 2, 4, 0, 5).reshape(12, 144)
    return ids[:, None, :], ids[:, :, None]


def body(
    latents, region_ids, attend_one, project_one, expand_one, reduce_one,
    merge_weight, attend_two, project_two, expand_two, reduce_two,
):
    tile = latents.reshape(2, 36, 4, 6, 512).transpose(1, 2, 0, 3, 4).reshape(36, 48, 512)
    reg_row, reg_col = window_ids(region_ids)
    in0 = jnp.concatenate(
        [attend_two.transpose(1, 0, 2).reshape(32, 768), jnp.concatenate([merge_weight[:, :512], merge_weight[:, 512:]], axis=0)],
        axis=1,
    )
    in1 = jnp.concatenate([expand_two, project_two.T], axis=1)
    in2 = reduce_two.T
    vmem = pl.BlockSpec(memory_space=pltpu.VMEM)
    hbm = pl.BlockSpec(memory_space=pl.ANY)
    sem = pltpu.SemaphoreType.DMA
    return pl.pallas_call(
        kernel,
        out_shape=jax.ShapeDtypeStruct((2, 72, 12, 256), BF),
        in_specs=[hbm] + [vmem] * 13 + [hbm] * 3,
        out_specs=hbm,
        scratch_shapes=[pltpu.VMEM((2, 4, 4, 4, 32, w), BF) for w in WIDTHS]
        + [
            pltpu.VMEM((39, 48, 512), BF), pltpu.VMEM((39, 16, 512), BF),
            pltpu.VMEM((39, 48, 512), BF), pltpu.VMEM((39, 16, 512), BF), pltpu.VMEM((36, 16, 512), BF),
            pltpu.VMEM((4, 432, 512), BF), pltpu.VMEM((432, 1024), BF), pltpu.VMEM((432, 768), BF),
            pltpu.VMEM((4, 432, 256), BF), pltpu.VMEM((432, 1024), BF), pltpu.VMEM((432, 1024), BF),
            pltpu.VMEM((432, 1024), F32), pltpu.VMEM((4, 2, 18, 12, 256), BF),
            sem((3, 24)), sem((3, 24)), sem((3, 16)), sem((3, 16)), sem((5,)),
            sem((3,)), sem((3,)), sem((8,)), sem((8,)), sem((3,)), sem((3,)),
        ],
        compiler_params=pltpu.CompilerParams(collective_id=0, has_side_effects=True, vmem_limit_bytes=63 * 2**20),
        cost_estimate=pl.CostEstimate(flops=24 * 10**9, bytes_accessed=10 * 10**6, transcendentals=10**7),
    )(
        tile, reg_row, reg_col, attend_one, project_one, expand_one, reduce_one, *choices(), in0, in1, in2
    )


def solution(mesh):
    return jax.shard_map(
        body,
        mesh=mesh,
        in_specs=(
            P(None, "lat", "lon", None), P(), P(), P(), P(), P(),
            P(("lon", "lat"), None), P(None, "lon", "lat"), P("lat", "lon"), P("lon", "lat"), P("lat", "lon"),
        ),
        out_specs=P(None, None, "lon", "lat"),
        check_vma=False,
    )
```

time: 696 us -> 162 us (0.23); the launches traced: 688 us -> 162 us
  waiting for transfers between devices: 321 us -> 0 us
  local copies, waits for them, and re-layouts: 206 us -> 11.8 us
  Pallas kernels: 0 us -> 149 us
  matrix products: 74.3 us -> 0 us
  blocking collectives: 44.8 us -> 0 us
  other arithmetic: 19.6 us -> 0.93 us
  between operations: 13.8 us -> 0.12 us
  starting transfers between devices: 8.55 us -> 0 us
    all_gather x5 -> x0, waiting for transfers between devices: 300 us -> none  [the longest x1 106 us: reduce_map(): lax.all_gather(weight_shard, 'lon', axis=1, tiled=True)]
    pallas_call x0 -> x1, Pallas kernels: none -> 149 us  [body(): pl.pallas_call(kernel, out_shape=jax.ShapeDtypeStruct((2, 72, 12, 256), B...]
    dot_general x10 -> x0, matrix products: 61.1 us -> none  [the longest x1 13.7 us: reduce_map(): jnp.dot(activated, lax.all_gather(weight_shard, 'lon', axis=1, tiled=True...]
    unnamed x33 -> x13, local copies, waits for them, and re-layouts: 61.8 us -> 3.59 us
    another operation x7 -> x2, local copies, waits for them, and re-layouts: 43.8 us -> 2.21 us  [window_ids(): return (ids[:, None, :], ids[:, :, None])]
    convert_element_type x5 -> x0, local copies, waits for them, and re-layouts: 33.8 us -> none  [the longest x1 13.4 us: tile_attention(): packed = jnp.einsum('abci,kio->abcko', normed, attend, preferred_element_...]
    all_gather x4 -> x0, blocking collectives: 29.4 us -> none  [the longest x1 8.94 us: body(): lax.all_gather(attend_two, 'lat', axis=2, tiled=True)]
    slice x10 -> x3, local copies, waits for them, and re-layouts: 23.6 us -> 0.17 us  [the longest x2 0.17 us: rows_of(): return jnp.concatenate([own[:, 3:], under], axis=1)]
  transfers between devices with their start and end apart: 9 -> 0, of which waited for: 7 -> 0; matrix products, arithmetic and copies ran while one was open for 33% -> 0% of each run, Pallas kernels for 0% -> 0%
where the time goes in v1:
time: 162 us
  Pallas kernels  149 us (92%)
  local copies, waits for them, and re-layouts  11.8 us (7%)
    pallas_call x1, Pallas kernels, body(): pl.pallas_call(kernel, out_shape=jax.ShapeDtypeStruct((2, 72, 12, 256), B...  149 us
    unnamed x13, local copies, waits for them, and re-layouts  3.59 us

profile of v1, /device:TPU:1, one launch (start us, length us, event | category | flops | bytes accessed | tf_op | source)
XLA Modules:
  0.0 161.6 jit_solution(13549214635512224064)
XLA Ops:
  0.0 0.0 copy-start
  0.0 3.4 %copy.32 = bf16[2,36,24,512]{3,0,2,1:T(2,128)(2,1)S(1)} copy(bf16[2,36,24,512]{3,2,1,0:T(8,128)(2,1)} %param.18) | data formatting | bytes 3538944 | tf_op args[0]
  3.4 1.0 copy.33
  4.4 1.8 %copy.41.tile = bf16[36,48,512]{2,1,0:T(8,128)(2,1)} copy(bf16[36,48,512]{2,0,1:T(8,128)(2,1)S(1)} %bitcast.12) | data formatting | bytes 3538944 | tf_op jit(solution)/shard_map/reshape | solution.py:490
  6.2 0.0 copy-start.3
  6.2 0.0 copy-start.2
  6.2 0.0 copy-start.1
  6.2 0.0 copy-start.4
  6.2 0.0 copy-done
  6.2 0.1 constant_dynamic-slice_fusion
  6.3 0.1 copy.46
  6.4 0.1 constant_dynamic-slice_fusion.1
  6.5 0.1 copy.45
  6.6 0.1 pad_add_fusion.2
  6.7 0.1 copy.36
  6.8 0.1 constant_dynamic-slice_fusion.2
  6.9 0.1 constant_dynamic-slice_fusion.3
  7.0 0.1 pad_add_fusion
  7.0 0.1 pad_add_fusion.1
  7.2 0.2 reshape.14
  7.3 0.1 copy.38
  7.4 0.8 broadcast_in_dim_reshape.6.reg_row
  8.2 1.4 broadcast_in_dim_reshape.8.reg_col
  9.6 0.0 copy-done.3
  9.6 0.0 copy-done.2
  9.7 0.0 copy-done.1
  9.7 0.0 copy-done.4
  9.7 0.7 maximum_maximum_fusion
  10.4 148.7 %shard_map.172 = bf16[2,72,12,256]{3,2,1,0:T(8,128)(2,1)} custom-call(bf16[36,48,512]{2,1,0:T(8,128)(2,1)} %copy.41.tile, s32[12,1,144]{2,1,0:T(1,128)} %broadcast_in_dim_reshape.6.reg_row, s32[12,144,1]{2,1,0:T(8,128)} %broadcast_in_dim_reshape.8.reg_col, bf16[3,512,512]{2,1,0:T(8,128)(2,1)} %attend.1, bf16[512,512]{1,0:T(8,128)(2,1)} %project.1, ...), custom_call_target="tpu_custom_call" | custom-call | flops 24000000000 | bytes 10000000 | tf_op jit(solution)/shard_map/pallas_call | solution.py:501
  159.1 2.5 %copy.43 = bf16[2,72,12,256]{3,1,2,0:T(8,128)(2,1)} copy(bf16[2,72,12,256]{3,2,1,0:T(8,128)(2,1)} %shard_map.172) | data formatting | bytes 1769472 | tf_op jit(solution)/shard_map/pallas_call | solution.py:501
  (3 shorter events, 0.0 us)
Async XLA Ops:
  0.0 6.2 %copy-start = (s32[2,144,768]{2,1,0:T(8,128)S(1)}, s32[2,144,768]{2,1,0:T(8,128)}, u32[]{:S(2)}) copy-start(s32[2,144,768]{2,1,0:T(8,128)} %param.19) | copy-start | bytes 2654212
  6.2 3.4 %copy-start.3 = (bf16[16,1024]{1,0:T(8,128)(2,1)S(1)}, bf16[16,1024]{1,0:T(8,128)(2,1)}, u32[]{:S(2)}) copy-start(bf16[16,1024]{1,0:T(8,128)(2,1)} %param.24) | copy-start | bytes 98308
  6.2 3.5 %copy-start.2 = (bf16[3,32,256]{2,1,0:T(8,128)(2,1)S(1)}, bf16[3,32,256]{2,1,0:T(8,128)(2,1)}, u32[]{:S(2)}) copy-start(bf16[3,32,256]{2,1,0:T(8,128)(2,1)} %param.25) | copy-start | bytes 147460
  6.2 3.5 %copy-start.1 = (bf16[32,1024]{1,0:T(8,128)(2,1)S(1)}, bf16[32,1024]{1,0:T(8,128)(2,1)}, u32[]{:S(2)}) copy-start(bf16[32,1024]{1,0:T(8,128)(2,1)} %param.27) | copy-start | bytes 196612
  6.2 3.5 %copy-start.4 = (bf16[256,32]{0,1:T(8,128)(2,1)S(1)}, bf16[256,32]{0,1:T(8,128)(2,1)}, u32[]{:S(2)}) copy-start(bf16[256,32]{0,1:T(8,128)(2,1)} %param.26) | copy-start | bytes 49156

commit v2 on v1

v2 whole, which is shorter than its diff:
```python
import jax
import jax.numpy as jnp
import numpy as np
from jax import lax
from jax.experimental import pallas as pl
from jax.experimental.pallas import tpu as pltpu
from jax.sharding import PartitionSpec as P

MESH = pl.DeviceIdType.MESH
BF = jnp.bfloat16
F32 = jnp.float32
EPSILON = 1e-05
MASKED = -1e30
ORDERS = (("x", "y", "z"), ("y", "z", "x"), ("z", "x", "y"))
WIDTHS = (1280, 2304)
SPANS = (((0, 384), (384, 512), (896, 384)), ((0, 640), (640, 768), (1408, 896)))
SUB = (0, -1, 1, 2)


def gather_plan(kind, buf, send, recv, sibs, sibr):
    lon = lax.axis_index("lon")
    lat = lax.axis_index("lat")
    me = {"x": (lon // 4) % 4, "y": lon % 4, "z": (lon // 16) * 2 + lat // 2}
    core = lat % 2

    def device(pos, c):
        return ((pos["z"] // 2) * 16 + pos["x"] * 4 + pos["y"], (pos["z"] % 2) * 2 + c)

    def shifted(axis, by):
        pos = dict(me)
        pos[axis] = (me[axis] + by + 4) % 4
        return pos

    def part(s, fix, half):
        at = [slice(None) if fix[a] is None else fix[a] for a in ("z", "x", "y")]
        rows = slice(None) if half is None else pl.ds(16 * half, 16)
        return buf.at[core, at[0], at[1], at[2], rows, pl.ds(*SPANS[kind][s])]

    def copy(s, n, fix, axis, by, half=None):
        ref = part(s, fix, half)
        return pltpu.make_async_remote_copy(
            src_ref=ref, dst_ref=ref, send_sem=send.at[3 * kind + s, n], recv_sem=recv.at[3 * kind + s, n],
            device_id=device(shifted(axis, by), core), device_id_type=MESH,
        )

    def sibling(s, k, j):
        ref = part(s, group(s, 3, SUB[k], SUB[j]), None)
        return pltpu.make_async_remote_copy(
            src_ref=ref, dst_ref=ref, send_sem=sibs.at[3 * kind + s, 4 * j + k], recv_sem=sibr.at[3 * kind + s, 4 * j + k],
            device_id=device(me, 1 - core), device_id_type=MESH,
        )

    def group(s, stage, second=0, third=0):
        axes = ORDERS[s]
        fix = dict(me)
        fix[axes[0]] = None
        fix[axes[1]] = (me[axes[1]] + second + 4) % 4
        fix[axes[2]] = (me[axes[2]] + third + 4) % 4
        return fix

    def own(s, by):
        fix = dict(me)
        axis = ORDERS[s][0]
        fix[axis] = (me[axis] + by + 4) % 4
        return fix

    def first(s):
        a = ORDERS[s][0]
        return copy(s, 0, own(s, 0), a, 1), copy(s, 1, own(s, 0), a, -1)

    def first_on(s):
        a = ORDERS[s][0]
        return copy(s, 2, own(s, -1), a, 1, 0), copy(s, 3, own(s, 1), a, -1, 1)

    def second(s):
        a = ORDERS[s][1]
        return copy(s, 4, group(s, 2), a, 1), copy(s, 5, group(s, 2), a, -1)

    def second_on(s):
        a = ORDERS[s][1]
        return copy(s, 6, group(s, 2, -1), a, 1, 0), copy(s, 7, group(s, 2, 1), a, -1, 1)

    def third(s, k):
        a = ORDERS[s][2]
        fix = group(s, 3, SUB[k])
        return copy(s, 8 + 4 * k, fix, a, 1), copy(s, 9 + 4 * k, fix, a, -1)

    def third_on(s, k):
        a = ORDERS[s][2]
        return (
            copy(s, 10 + 4 * k, group(s, 3, SUB[k], -1), a, 1, 0),
            copy(s, 11 + 4 * k, group(s, 3, SUB[k], 1), a, -1, 1),
        )

    def go(copies):
        for c in copies:
            c.start()

    def got(copies):
        for c in copies:
            c.wait_recv()

    streams = range(3)

    def e0():
        for s in streams:
            go(first(s))

    def e1():
        for s in streams:
            got(first(s))
            go(first_on(s))

    def e2():
        for s in streams:
            got(first_on(s))
            go(second(s))
            go(third(s, 0))
        for s in streams:
            sibling(s, 0, 0).start()

    def e3():
        for s in streams:
            got(second(s))
            go(second_on(s))
            go(third(s, 1))
            go(third(s, 2))
        for s in streams:
            sibling(s, 1, 0).start()
            sibling(s, 2, 0).start()
        for s in streams:
            got(third(s, 0))
            go(third_on(s, 0))
            sibling(s, 0, 1).start()
            sibling(s, 0, 2).start()

    def e4():
        for s in streams:
            got(second_on(s))
            go(third(s, 3))
            sibling(s, 3, 0).start()
        for k in (1, 2):
            for s in streams:
                got(third(s, k))
                go(third_on(s, k))
                sibling(s, k, 1).start()
                sibling(s, k, 2).start()

    def e5():
        for s in streams:
            got(third_on(s, 0))
            sibling(s, 0, 3).start()
        for s in streams:
            got(third(s, 3))
            go(third_on(s, 3))
            sibling(s, 3, 1).start()
            sibling(s, 3, 2).start()

    def e6():
        for k in (1, 2):
            for s in streams:
                got(third_on(s, k))
                sibling(s, k, 3).start()

    def e7():
        for s in streams:
            got(third_on(s, 3))
            sibling(s, 3, 3).start()

    def arrived(which):
        for j in range(4):
            for k in range(4):
                for s in which:
                    sibling(s, k, j).wait_recv()

    def drain():
        for s in streams:
            for c in first(s) + first_on(s) + second(s) + second_on(s):
                c.wait_send()
            for k in range(4):
                for c in third(s, k) + third_on(s, k):
                    c.wait_send()
                for j in range(4):
                    sibling(s, k, j).wait_send()

    partners = [device(shifted(a, d), core) for a in "xyz" for d in (1, -1)] + [device(me, 1 - core)]
    return me, core, (e0, e1, e2, e3, e4, e5, e6, e7), arrived, drain, partners


def normed(values):
    centered = values - jnp.mean(values, axis=-1, keepdims=True)
    variance = jnp.mean(centered * centered, axis=-1, keepdims=True)
    return centered * lax.rsqrt(variance + EPSILON)


def gelu(v):
    return 0.5 * v * (1.0 + jnp.tanh(0.7978845608028654 * (v + 0.044715 * (v * v * v))))


def mm(a, b):
    return jnp.dot(a, b, preferred_element_type=F32)


def mm_nt(a, b):
    return lax.dot_general(a, b, (((1,), (1,)), ((), ())), preferred_element_type=F32)


def attend_heads(pairs):
    is_low = lax.broadcasted_iota(jnp.int32, pairs[0][0].shape, 1) < 64
    low_f = (lax.broadcasted_iota(jnp.int32, pairs[0][1].shape, 1) < 64).astype(F32)
    low = low_f.astype(BF)
    high = (1.0 - low_f).astype(BF)
    scores = []
    for q, k, _, bias in pairs:
        for mask in (low, high):
            s = mm_nt(q, k * mask)
            scores.append(s if bias is None else s + bias)
    highest = [jnp.max(s, axis=-1, keepdims=True) for s in scores]
    lifted = [jnp.exp(s - m).astype(BF) for s, m in zip(scores, highest)]
    blends = []
    for n, (_, _, v, _) in enumerate(pairs):
        blends.append((mm(lifted[2 * n], v * low + high), mm(lifted[2 * n + 1], v * high + low)))
    outs = []
    for even, odd in blends:
        sums = pltpu.roll(jnp.where(is_low, odd, even), 64, 1)
        outs.append(jnp.where(is_low, even, odd) / sums)
    return outs


def kernel(
    latents, ids, attend_h, project_h, expand_h, shrink_h, merge_h, attend2_h, project2_h, expand2_h, reduce2_h,
    pick_own_h, pick_side_h, put_h, quarter_h, mix_h, pad_h,
    out,
    b0, b1, tile, edge_w, edge_e, cols_w, cols_e, y_rows, quart, merged, qkv, blend, norm2, total, lifted, result,
    attend, project, expand, shrink, pick_own, pick_side, put, quarter, mix, pad,
    send, recv, sibs, sibr, loc, wsem, halo_s, halo_r, fin_s, fin_r,
):
    me, core, first_events, first_arrived, first_drain, partners = gather_plan(0, b0, send, recv, sibs, sibr)
    _, _, later_events, later_arrived, later_drain, _ = gather_plan(1, b1, send, recv, sibs, sibr)
    lon = lax.axis_index("lon")
    lat = lax.axis_index("lat")
    west, east = (lon + 31) % 32, (lon + 1) % 32
    above, below = (lat + 3) % 4, (lat + 1) % 4

    fetch_tile = pltpu.make_async_copy(latents, tile.at[:, pl.ds(3, 36)], loc.at[0])
    fetch_tile.start()
    at = (core, me["z"], me["x"], me["y"])
    shards = [
        (merge_h.at[:, pl.ds(0, 512)], b0.at[at + (pl.ds(0, 16), pl.ds(768, 512))]),
        (merge_h.at[:, pl.ds(512, 512)], b0.at[at + (pl.ds(16, 16), pl.ds(768, 512))]),
    ]
    shards += [(attend2_h.at[i], b0.at[at + (slice(None), pl.ds(256 * i, 256))]) for i in range(3)]
    shards += [
        (project2_h, b1.at[at + (slice(None), pl.ds(0, 256))]),
        (expand2_h, b1.at[at + (slice(None), pl.ds(256, 1024))]),
        (reduce2_h, b1.at[at + (slice(None), pl.ds(1280, 1024))]),
    ]
    shards = [pltpu.make_async_copy(src, dst, loc.at[n + 1]) for n, (src, dst) in enumerate(shards)]
    for c in shards:
        c.start()
    weights = [
        pltpu.make_async_copy(src, dst, wsem.at[n])
        for n, (src, dst) in enumerate(
            (
                (pick_own_h, pick_own), (pick_side_h, pick_side), (attend_h, attend), (project_h, project), (expand_h, expand),
                (shrink_h, shrink), (put_h, put), (quarter_h, quarter), (mix_h, mix), (pad_h, pad),
            )
        )
    ]
    for c in weights:
        c.start()
    everyone = partners + [(west, lat), (east, lat), (lon, above), (lon, below), (lon, (lat + 2) % 4)]
    everyone += [(west, above), (east, below), (west, below), (east, above)]
    barrier = pltpu.get_barrier_semaphore()
    for d in everyone:
        pl.semaphore_signal(barrier, inc=1, device_id=d, device_id_type=MESH)
    fetch_tile.wait()
    for level in range(2):
        edge_w[:, pl.ds(8 * level, 8)] = tile[level, pl.ds(3, 36), pl.ds(0, 8)]
        edge_e[:, pl.ds(8 * level, 8)] = tile[level, pl.ds(3, 36), pl.ds(16, 8)]
    for c in shards:
        c.wait()
    pl.semaphore_wait(barrier, len(everyone))

    def remote(src, dst, ssem, rsem, to):
        return pltpu.make_async_remote_copy(
            src_ref=src, dst_ref=dst, send_sem=ssem, recv_sem=rsem, device_id=to, device_id_type=MESH
        )

    def halo(n, src, dst, to):
        return remote(src, dst, halo_s.at[n], halo_r.at[n], to)

    def sides(a):
        here, there = pl.ds(6 * a - 3, 6), pl.ds(6 * a, 6)
        return [
            halo(2 * a - 2, edge_w.at[here], cols_e.at[there], (west, lat)),
            halo(2 * a - 1, edge_e.at[here], cols_w.at[there], (east, lat)),
        ]

    top, low = pl.ds(0, 3), pl.ds(33, 3)
    before, after = pl.ds(0, 3), pl.ds(39, 3)
    rim = [
        halo(10, edge_w.at[top], cols_e.at[pl.ds(3, 3)], (west, lat)),
        halo(11, edge_e.at[top], cols_w.at[pl.ds(3, 3)], (east, lat)),
        halo(12, edge_w.at[low], cols_e.at[pl.ds(36, 3)], (west, lat)),
        halo(13, edge_e.at[low], cols_w.at[pl.ds(36, 3)], (east, lat)),
        halo(14, edge_w.at[top], cols_e.at[after], (west, above)),
        halo(15, edge_e.at[top], cols_w.at[after], (east, above)),
        halo(16, edge_w.at[low], cols_e.at[before], (west, below)),
        halo(17, edge_e.at[low], cols_w.at[before], (east, below)),
        halo(18, latents.at[:, top], tile.at[:, after], (lon, above)),
        halo(19, latents.at[:, low], tile.at[:, before], (lon, below)),
    ]
    first_events[0]()
    for a in (1, 2):
        for c in sides(a):
            c.start()
    later_events[0]()
    for c in sides(3):
        c.start()
    for c in weights:
        c.wait()

    early = {
        (0, 0): (first_events[1], later_events[1]), (0, 2): (first_events[2],),
        (1, 1): (first_events[3],), (1, 2): (later_events[2],),
        (2, 1): (first_events[4],), (2, 2): (later_events[3],),
        (3, 1): (first_events[5],), (3, 2): (first_events[6],),
        (4, 0): (later_events[4],), (4, 1): (first_events[7],), (5, 1): (later_events[5],),
    }

    def step_events(t, half):
        for (when, which), events in early.items():
            if which == half:

                @pl.when(t == when)
                def _(events=events):
                    for event in events:
                        event()

    def strip(t, carry):
        a = jnp.where(t < 5, t + 1, (t - 5) * 6)

        @pl.when(t < 5)
        def _():
            for c in sides(t + 1):
                c.wait_recv()

        @pl.when(t == 5)
        def _():
            for c in rim:
                c.wait_recv()

        span = pl.ds(6 * a, 6)
        own = tile[:, span].astype(F32).reshape(288, 512).astype(BF)
        side = jnp.concatenate([cols_w[span].reshape(96, 512), cols_e[span].reshape(96, 512)], axis=0)
        x = mm(pick_own[...], own) + mm(pick_side[...], side)
        n = normed(x).astype(BF)
        q = (mm(n[:360], attend[0]) * 0.125).astype(BF)
        k = mm(n, attend[1]).astype(BF)
        v = mm(n, attend[2]).astype(BF)
        parts = []
        for b, size in enumerate((72, 144, 72)):
            kinds = lax.broadcasted_iota(jnp.int32, (16, 144), 0)
            hot = (ids[pl.ds(3 * a + b, 1), :] == kinds).astype(F32).astype(BF)
            same = lax.dot_general(hot, hot, (((0,), (0,)), ((), ())), preferred_element_type=F32)
            bias = ((same - 1.0) * -MASKED)[:size]
            r = slice(144 * b, 144 * b + 144)
            r_q = slice(144 * b, 144 * b + size)
            heads = [(q[r_q, c : c + 128], k[r, c : c + 128], v[r, c : c + 128], bias) for c in range(0, 512, 128)]
            parts.append(jnp.concatenate(attend_heads(heads), axis=1))
        o = jnp.concatenate(parts, axis=0).astype(BF)
        x = jnp.concatenate([x[:72], x[144:360]], axis=0)
        step_events(t, 0)
        for when in range(2):

            @pl.when(t == when)
            def _(when=when):
                for c in sides(when + 4):
                    c.start()

        @pl.when(t == 2)
        def _():
            for c in rim:
                c.start()

        hid = (x + mm(o, project[...])).astype(BF)
        hid_f = hid.astype(F32)
        n = normed(hid_f).astype(BF)
        acc = hid_f
        for c in range(4):
            u = gelu(mm(n, expand[:, 512 * c : 512 * c + 512])).astype(BF)
            acc = acc + mm(u, shrink[512 * c : 512 * c + 512, :])
            if c == 1:
                step_events(t, 1)
        y_rows[span] = mm(put[...], acc.astype(BF)).astype(BF).reshape(6, 48, 512)
        step_events(t, 2)
        return carry

    lax.fori_loop(0, 7, strip, 0)

    for w in range(3):
        both = y_rows[pl.ds(12 * w + 3, 12)].reshape(6, 2, 48, 512)
        found = [mm(quarter[...], both[:, odd].reshape(288, 512)) for odd in range(2)]
        quads = [found[0][:144], found[1][:144], found[0][144:], found[1][144:]]
        mean = sum(jnp.sum(p, axis=-1, keepdims=True) for p in quads) * (1.0 / 2048.0)
        quads = [p - mean for p in quads]
        variance = sum(jnp.sum(p * p, axis=-1, keepdims=True) for p in quads) * (1.0 / 2048.0)
        scale = lax.rsqrt(variance + EPSILON)
        for p in range(4):
            quart[p, pl.ds(144 * w, 144)] = mm((quads[p] * scale).astype(BF), mix[...]).astype(BF)

    later_events[6]()
    first_arrived(range(3))
    for half in range(2):
        acc = jnp.zeros((432, 512), F32)
        for z in range(4):
            for c in range(2):
                ch = slice(128 * ((z % 2) * 2 + c), 128 * ((z % 2) * 2 + c) + 128)
                left = jnp.concatenate([quart[z // 2 * 2, :, ch], quart[z // 2 * 2 + 1, :, ch]], axis=1)
                right = b0[c, z, :, :, pl.ds(16 * half, 16), pl.ds(768, 512)].reshape(256, 512)
                acc = acc + mm(left, right)
        merged[:, pl.ds(512 * half, 512)] = acc.astype(BF)

    norm2[...] = normed(merged[...].astype(F32)).astype(BF)

    def attend_slice(g, carry):
        z_lo, c = g // 2, g % 2
        acc = mm(norm2[:, pl.ds(0, 512)], b0[c, z_lo, :, :, :, pl.ds(0, 768)].reshape(512, 768))
        acc = acc + mm(norm2[:, pl.ds(512, 512)], b0[c, z_lo + 2, :, :, :, pl.ds(0, 768)].reshape(512, 768))
        qkv[:, pl.ds(0, 256)] = (acc[:, :256] * 0.125).astype(BF)
        qkv[:, pl.ds(256, 512)] = acc[:, 256:].astype(BF)
        spots = [(pl.ds(144 * w, 144), 128 * h) for w in range(3) for h in range(2)]
        heads = [(qkv[r, pl.ds(c, 128)], qkv[r, pl.ds(256 + c, 128)], qkv[r, pl.ds(512 + c, 128)], None) for r, c in spots]
        for (r, c), o in zip(spots, attend_heads(heads)):
            blend[g, r, pl.ds(c, 128)] = o.astype(BF)

        @pl.when(g == 0)
        def _():
            later_events[7]()

        return carry

    lax.fori_loop(0, 4, attend_slice, 0)

    later_arrived((0, 1))
    for half in range(2):
        acc = merged[:, pl.ds(512 * half, 512)].astype(F32)
        for g in range(4):
            w_t = b1[g % 2, 2 * half + g // 2, :, :, :, pl.ds(0, 256)].reshape(512, 256)
            acc = acc + mm_nt(blend[g], w_t)
        acc = acc.astype(BF).astype(F32)
        total[2 * half] = acc[:, :256]
        total[2 * half + 1] = acc[:, 256:]
    norm2[...] = normed(jnp.concatenate([total[p] for p in range(4)], axis=1)).astype(BF)

    def widen(g, carry):
        z_lo, c = g // 2, g % 2
        u = mm(norm2[:, pl.ds(0, 512)], b1[c, z_lo, :, :, :, pl.ds(256, 1024)].reshape(512, 1024))
        u = u + mm(norm2[:, pl.ds(512, 512)], b1[c, z_lo + 2, :, :, :, pl.ds(256, 1024)].reshape(512, 1024))
        lifted[g] = gelu(u).astype(BF)
        return carry

    lax.fori_loop(0, 4, widen, 0)
    later_arrived((2,))

    mine = out.at[:, pl.ds(18 * lat, 18)]
    owners = ((lat + 2) % 4, 3 - lat, (lat // 2) * 2 + 1 - core, lat)

    def hand_out(n):
        src = result.at[owners[n]]
        if n == 3:
            return pltpu.make_async_copy(src, mine, loc.at[9])
        return remote(src, mine, fin_s.at[n], fin_r.at[n], (lon, owners[n]))

    for n in range(4):
        p = owners[n]
        acc = total[p]
        for g in range(4):
            back = b1[g % 2, g // 2 + 2 * (p // 2), pl.ds(p % 2 * 2, 2), :, :, pl.ds(1280, 1024)].reshape(256, 1024)
            acc = acc + mm_nt(lifted[g], back)
        acc = acc.astype(BF)
        for w in range(3):
            spread = mm(pad[...], acc[144 * w : 144 * w + 144]).astype(BF).reshape(12, 16, 256)
            for level in range(2):
                result[p, level, pl.ds(6 * w, 6)] = spread[6 * level : 6 * level + 6, :12]
        hand_out(n).start()

    first_drain()
    later_drain()
    for c in rim + [c for a in range(1, 6) for c in sides(a)]:
        c.wait_send()
    for n in range(4):
        hand_out(n).wait()


def choose(shape, pairs):
    out = np.zeros(shape, np.float32)
    for r, c in pairs:
        out[r, c] = 1.0
    return jnp.asarray(out, BF)


def choices():
    own, side, put, quarter = [], [], [], []
    for n, h in enumerate((0, -1, 1, 2, 3, 4)):
        for rho in range(6):
            for level in range(2):
                for c in range(6):
                    i = n * 72 + rho * 12 + level * 6 + c
                    if h < 0:
                        side.append((i, rho * 16 + level * 8 + c + 2))
                    elif h > 3:
                        side.append((i, 96 + rho * 16 + level * 8 + c))
                    else:
                        own.append((i, level * 144 + rho * 24 + h * 6 + c))
                        put.append((rho * 48 + h * 12 + level * 6 + c, h * 72 + rho * 12 + level * 6 + c))
    for pc in range(2):
        for level in range(2):
            for ii in range(6):
                for j in range(12):
                    h, c = divmod(2 * j + pc, 6)
                    quarter.append((pc * 144 + level * 72 + ii * 12 + j, ii * 48 + h * 12 + level * 6 + c))
    mix = [(blk * 64 + g * 16 + r, g * 128 + blk * 16 + r) for g in range(4) for blk in range(8) for r in range(16)]
    pad = [(g * 16 + j, g * 12 + j) for g in range(12) for j in range(12)]
    return (
        choose((432, 288), own), choose((432, 192), side), choose((288, 288), put),
        choose((288, 288), quarter), choose((512, 512), mix), choose((192, 144), pad),
    )


def window_ids(region_ids):
    lat = lax.axis_index("lat")
    lon = lax.axis_index("lon")

    def around(field, axis, place, count, size, edge):
        def cut(at, start, width):
            return lax.dynamic_slice_in_dim(field, at % count * size + start, width, axis)

        return [cut(place - 1, size - edge, edge), cut(place, 0, size), cut(place + 1, 0, edge)]

    field = jnp.concatenate(around(region_ids, 1, lat + 4, 4, 36, 3), axis=1)
    before, own, after = around(field, 2, lon + 32, 32, 24, 6)
    ids = jnp.concatenate([own[:, :, :6], before, own[:, :, 6:], after], axis=2)
    return ids.reshape(2, 7, 6, 3, 2, 6).transpose(1, 3, 4, 2, 0, 5).reshape(21, 144)


def body(
    latents, region_ids, attend_one, project_one, expand_one, reduce_one,
    merge_weight, attend_two, project_two, expand_two, reduce_two,
):
    vmem = pl.BlockSpec(memory_space=pltpu.VMEM)
    hbm = pl.BlockSpec(memory_space=pl.ANY)
    sem = pltpu.SemaphoreType.DMA
    regroup = choices()
    return pl.pallas_call(
        kernel,
        out_shape=jax.ShapeDtypeStruct((2, 72, 12, 256), BF),
        in_specs=[hbm, vmem] + [hbm] * 15,
        out_specs=hbm,
        scratch_shapes=[pltpu.VMEM((2, 4, 4, 4, 32, w), BF) for w in WIDTHS]
        + [
            pltpu.VMEM((2, 42, 24, 512), BF), pltpu.VMEM((36, 16, 512), BF), pltpu.VMEM((36, 16, 512), BF),
            pltpu.VMEM((42, 16, 512), BF), pltpu.VMEM((42, 16, 512), BF), pltpu.VMEM((42, 48, 512), BF),
            pltpu.VMEM((4, 432, 512), BF), pltpu.VMEM((432, 1024), BF), pltpu.VMEM((432, 768), BF),
            pltpu.VMEM((4, 432, 256), BF), pltpu.VMEM((432, 1024), BF),
            pltpu.VMEM((4, 432, 256), F32), pltpu.VMEM((4, 432, 1024), BF), pltpu.VMEM((4, 2, 18, 12, 256), BF),
            pltpu.VMEM((3, 512, 512), BF), pltpu.VMEM((512, 512), BF),
            pltpu.VMEM((512, 2048), BF), pltpu.VMEM((2048, 512), BF),
        ]
        + [pltpu.VMEM(m.shape, BF) for m in regroup]
        + [
            sem((6, 24)), sem((6, 24)), sem((6, 16)), sem((6, 16)), sem((12,)), sem((10,)),
            sem((20,)), sem((20,)), sem((3,)), sem((3,)),
        ],
        compiler_params=pltpu.CompilerParams(collective_id=0, has_side_effects=True, vmem_limit_bytes=63 * 2**20),
        cost_estimate=pl.CostEstimate(flops=24 * 10**9, bytes_accessed=10 * 10**6, transcendentals=10**7),
    )(
        latents, window_ids(region_ids), attend_one, project_one, expand_one, reduce_one,
        merge_weight, attend_two, project_two.T, expand_two, reduce_two.T, *regroup,
    )


def solution(mesh):
    return jax.shard_map(
        body,
        mesh=mesh,
        in_specs=(
            P(None, "lat", "lon", None), P(), P(), P(), P(), P(),
            P(("lon", "lat"), None), P(None, "lon", "lat"), P("lat", "lon"), P("lon", "lat"), P("lat", "lon"),
        ),
        out_specs=P(None, None, "lon", "lat"),
        check_vma=False,
    )
```

time: 162 us -> 133 us (0.82)
  Pallas kernels: 149 us -> 126 us
  local copies, waits for them, and re-layouts: 11.8 us -> 5.79 us
    pallas_call x1, Pallas kernels: 149 us -> 126 us  [body(): pl.pallas_call(kernel, out_shape=jax.ShapeDtypeStruct((2, 72, 12, 256), B...]
    unnamed x13 -> x0, local copies, waits for them, and re-layouts: 3.59 us -> none
    another operation x2 -> x0, local copies, waits for them, and re-layouts: 2.21 us -> none  [window_ids(): return (ids[:, None, :], ids[:, :, None])]
    dynamic_slice x2, local copies, waits for them, and re-layouts: 0.17 us -> 1.83 us  [cut(): lax.dynamic_slice_in_dim(field, at % count * size + start, width, axis)]
where the time goes in v2:
time: 133 us; the launch traced here: 132 us
  Pallas kernels  126 us (95%)
  local copies, waits for them, and re-layouts  5.79 us (4%)
    pallas_call x1, Pallas kernels, body(): pl.pallas_call(kernel, out_shape=jax.ShapeDtypeStruct((2, 72, 12, 256), B...  126 us

profile of v2, /device:TPU:1, one launch (start us, length us, event | category | flops | bytes accessed | tf_op | source)
XLA Modules:
  0.0 131.7 jit_solution(6525576920177394846)
XLA Ops:
  0.0 0.8 constant_dynamic-slice_fusion.6
  0.8 1.0 constant_dynamic-slice_fusion.5
  1.9 0.1 constant_dynamic-slice_fusion.3
  2.0 0.1 constant_dynamic-slice_fusion
  2.1 0.1 pad_add_fusion.1
  2.2 0.2 reshape.6
  2.5 0.1 copy.21
  2.6 0.9 reshape.7.ids
  3.5 125.7 %shard_map.163 = bf16[2,72,12,256]{3,2,1,0:T(8,128)(2,1)} custom-call(bf16[2,36,24,512]{3,2,1,0:T(8,128)(2,1)} %latents.1, s32[21,144]{1,0:T(8,128)} %reshape.7.ids, bf16[3,512,512]{2,1,0:T(8,128)(2,1)} %attend_h.1, bf16[512,512]{1,0:T(8,128)(2,1)} %project_h.1, bf16[512,2048]{1,0:T(8,128)(2,1)} %expand_h.1, bf16[2048,512]{1,0:T(8,128)(2,1)} %shrink_h.1, ...), custom_call_target="tpu_custom_call" | custom-call | flops 24000000000 | bytes 10000000 | tf_op jit(solution)/shard_map/pallas_call | solution.py:556
  129.3 2.5 %copy.22 = bf16[2,72,12,256]{3,1,2,0:T(8,128)(2,1)} copy(bf16[2,72,12,256]{3,2,1,0:T(8,128)(2,1)} %shard_map.163) | data formatting | bytes 1769472 | tf_op jit(solution)/shard_map/pallas_call | solution.py:556
  (2 shorter events, 0.1 us)

commit v3 on v2

--- a/solution.py
+++ b/solution.py
@@ -12,8 +12,8 @@
 EPSILON = 1e-05
 MASKED = -1e30
 ORDERS = (("x", "y", "z"), ("y", "z", "x"), ("z", "x", "y"))
-WIDTHS = (1280, 2304)
-SPANS = (((0, 384), (384, 512), (896, 384)), ((0, 640), (640, 768), (1408, 896)))
+WIDTHS = (2560, 1024)
+SPANS = (((0, 896), (896, 896), (1792, 768)), ((0, 256), (256, 384), (640, 384)))
 SUB = (0, -1, 1, 2)
 
 
@@ -167,10 +167,10 @@
             got(third_on(s, 3))
             sibling(s, 3, 3).start()
 
-    def arrived(which):
+    def arrived():
         for j in range(4):
             for k in range(4):
-                for s in which:
+                for s in streams:
                     sibling(s, k, j).wait_recv()
 
     def drain():
@@ -236,7 +236,7 @@
     send, recv, sibs, sibr, loc, wsem, halo_s, halo_r, fin_s, fin_r,
 ):
     me, core, first_events, first_arrived, first_drain, partners = gather_plan(0, b0, send, recv, sibs, sibr)
-    _, _, later_events, later_arrived, later_drain, _ = gather_plan(1, b1, send, recv, sibs, sibr)
+    _, _, last_events, last_arrived, last_drain, _ = gather_plan(1, b1, send, recv, sibs, sibr)
     lon = lax.axis_index("lon")
     lat = lax.axis_index("lat")
     west, east = (lon + 31) % 32, (lon + 1) % 32
@@ -251,9 +251,9 @@
     ]
     shards += [(attend2_h.at[i], b0.at[at + (slice(None), pl.ds(256 * i, 256))]) for i in range(3)]
     shards += [
-        (project2_h, b1.at[at + (slice(None), pl.ds(0, 256))]),
-        (expand2_h, b1.at[at + (slice(None), pl.ds(256, 1024))]),
-        (reduce2_h, b1.at[at + (slice(None), pl.ds(1280, 1024))]),
+        (project2_h, b0.at[at + (slice(None), pl.ds(1280, 256))]),
+        (expand2_h, b0.at[at + (slice(None), pl.ds(1536, 1024))]),
+        (reduce2_h, b1.at[at]),
     ]
     shards = [pltpu.make_async_copy(src, dst, loc.at[n + 1]) for n, (src, dst) in enumerate(shards)]
     for c in shards:
@@ -315,18 +315,16 @@
     for a in (1, 2):
         for c in sides(a):
             c.start()
-    later_events[0]()
+    last_events[0]()
     for c in sides(3):
         c.start()
     for c in weights:
         c.wait()
 
+    f, r = first_events, last_events
     early = {
-        (0, 0): (first_events[1], later_events[1]), (0, 2): (first_events[2],),
-        (1, 1): (first_events[3],), (1, 2): (later_events[2],),
-        (2, 1): (first_events[4],), (2, 2): (later_events[3],),
-        (3, 1): (first_events[5],), (3, 2): (first_events[6],),
-        (4, 0): (later_events[4],), (4, 1): (first_events[7],), (5, 1): (later_events[5],),
+        (0, 0): (f[1],), (0, 1): (r[1],), (0, 3): (f[2],), (1, 3): (f[3],), (3, 0): (f[4],), (4, 1): (f[5],),
+        (5, 0): (r[2],), (5, 1): (f[6],), (6, 1): (r[3],), (6, 3): (f[7],),
     }
 
     def step_events(t, half):
@@ -359,6 +357,7 @@
         q = (mm(n[:360], attend[0]) * 0.125).astype(BF)
         k = mm(n, attend[1]).astype(BF)
         v = mm(n, attend[2]).astype(BF)
+        step_events(t, 0)
         parts = []
         for b, size in enumerate((72, 144, 72)):
             kinds = lax.broadcasted_iota(jnp.int32, (16, 144), 0)
@@ -371,7 +370,7 @@
             parts.append(jnp.concatenate(attend_heads(heads), axis=1))
         o = jnp.concatenate(parts, axis=0).astype(BF)
         x = jnp.concatenate([x[:72], x[144:360]], axis=0)
-        step_events(t, 0)
+        step_events(t, 1)
         for when in range(2):
 
             @pl.when(t == when)
@@ -392,9 +391,9 @@
             u = gelu(mm(n, expand[:, 512 * c : 512 * c + 512])).astype(BF)
             acc = acc + mm(u, shrink[512 * c : 512 * c + 512, :])
             if c == 1:
-                step_events(t, 1)
+                step_events(t, 2)
         y_rows[span] = mm(put[...], acc.astype(BF)).astype(BF).reshape(6, 48, 512)
-        step_events(t, 2)
+        step_events(t, 3)
         return carry
 
     lax.fori_loop(0, 7, strip, 0)
@@ -410,8 +409,7 @@
         for p in range(4):
             quart[p, pl.ds(144 * w, 144)] = mm((quads[p] * scale).astype(BF), mix[...]).astype(BF)
 
-    later_events[6]()
-    first_arrived(range(3))
+    first_arrived()
     for half in range(2):
         acc = jnp.zeros((432, 512), F32)
         for z in range(4):
@@ -422,6 +420,7 @@
                 acc = acc + mm(left, right)
         merged[:, pl.ds(512 * half, 512)] = acc.astype(BF)
 
+    last_events[4]()
     norm2[...] = normed(merged[...].astype(F32)).astype(BF)
 
     def attend_slice(g, carry):
@@ -435,19 +434,22 @@
         for (r, c), o in zip(spots, attend_heads(heads)):
             blend[g, r, pl.ds(c, 128)] = o.astype(BF)
 
-        @pl.when(g == 0)
+        @pl.when(g == 1)
         def _():
-            later_events[7]()
+            last_events[5]()
+
+        @pl.when(g == 3)
+        def _():
+            last_events[6]()
 
         return carry
 
     lax.fori_loop(0, 4, attend_slice, 0)
 
-    later_arrived((0, 1))
     for half in range(2):
         acc = merged[:, pl.ds(512 * half, 512)].astype(F32)
         for g in range(4):
-            w_t = b1[g % 2, 2 * half + g // 2, :, :, :, pl.ds(0, 256)].reshape(512, 256)
+            w_t = b0[g % 2, 2 * half + g // 2, :, :, :, pl.ds(1280, 256)].reshape(512, 256)
             acc = acc + mm_nt(blend[g], w_t)
         acc = acc.astype(BF).astype(F32)
         total[2 * half] = acc[:, :256]
@@ -456,13 +458,14 @@
 
     def widen(g, carry):
         z_lo, c = g // 2, g % 2
-        u = mm(norm2[:, pl.ds(0, 512)], b1[c, z_lo, :, :, :, pl.ds(256, 1024)].reshape(512, 1024))
-        u = u + mm(norm2[:, pl.ds(512, 512)], b1[c, z_lo + 2, :, :, :, pl.ds(256, 1024)].reshape(512, 1024))
+        u = mm(norm2[:, pl.ds(0, 512)], b0[c, z_lo, :, :, :, pl.ds(1536, 1024)].reshape(512, 1024))
+        u = u + mm(norm2[:, pl.ds(512, 512)], b0[c, z_lo + 2, :, :, :, pl.ds(1536, 1024)].reshape(512, 1024))
         lifted[g] = gelu(u).astype(BF)
         return carry
 
     lax.fori_loop(0, 4, widen, 0)
-    later_arrived((2,))
+    last_events[7]()
+    last_arrived()
 
     mine = out.at[:, pl.ds(18 * lat, 18)]
     owners = ((lat + 2) % 4, 3 - lat, (lat // 2) * 2 + 1 - core, lat)
@@ -477,7 +480,7 @@
         p = owners[n]
         acc = total[p]
         for g in range(4):
-            back = b1[g % 2, g // 2 + 2 * (p // 2), pl.ds(p % 2 * 2, 2), :, :, pl.ds(1280, 1024)].reshape(256, 1024)
+            back = b1[g % 2, g // 2 + 2 * (p // 2), pl.ds(p % 2 * 2, 2)].reshape(256, 1024)
             acc = acc + mm_nt(lifted[g], back)
         acc = acc.astype(BF)
         for w in range(3):
@@ -487,7 +490,7 @@
         hand_out(n).start()
 
     first_drain()
-    later_drain()
+    last_drain()
     for c in rim + [c for a in range(1, 6) for c in sides(a)]:
         c.wait_send()
     for n in range(4):

time: 133 us -> 129 us (0.970); the launches traced: 132 us -> 129 us
  Pallas kernels: 126 us -> 123 us
    pallas_call x1, Pallas kernels: 126 us -> 123 us  [body(): pl.pallas_call(kernel, out_shape=jax.ShapeDtypeStruct((2, 72, 12, 256), B...]
where the time goes in v3:
time: 129 us
  Pallas kernels  123 us (95%)
  local copies, waits for them, and re-layouts  5.79 us (4%)
    pallas_call x1, Pallas kernels, body(): pl.pallas_call(kernel, out_shape=jax.ShapeDtypeStruct((2, 72, 12, 256), B...  123 us

profile of v3, /device:TPU:1, one launch (start us, length us, event | category | flops | bytes accessed | tf_op | source)
XLA Modules:
  0.0 129.1 jit_solution(16981090511664013381)
XLA Ops:
  0.0 0.8 constant_dynamic-slice_fusion.6
  0.8 1.0 constant_dynamic-slice_fusion.5
  1.9 0.1 constant_dynamic-slice_fusion.3
  2.0 0.1 constant_dynamic-slice_fusion
  2.1 0.1 pad_add_fusion.1
  2.2 0.2 reshape.6
  2.5 0.1 copy.21
  2.6 0.9 reshape.7.ids
  3.5 123.1 %shard_map.163 = bf16[2,72,12,256]{3,2,1,0:T(8,128)(2,1)} custom-call(bf16[2,36,24,512]{3,2,1,0:T(8,128)(2,1)} %latents.1, s32[21,144]{1,0:T(8,128)} %reshape.7.ids, bf16[3,512,512]{2,1,0:T(8,128)(2,1)} %attend_h.1, bf16[512,512]{1,0:T(8,128)(2,1)} %project_h.1, bf16[512,2048]{1,0:T(8,128)(2,1)} %expand_h.1, bf16[2048,512]{1,0:T(8,128)(2,1)} %shrink_h.1, ...), custom_call_target="tpu_custom_call" | custom-call | flops 24000000000 | bytes 10000000 | tf_op jit(solution)/shard_map/pallas_call | solution.py:559
  126.6 2.5 %copy.22 = bf16[2,72,12,256]{3,1,2,0:T(8,128)(2,1)} copy(bf16[2,72,12,256]{3,2,1,0:T(8,128)(2,1)} %shard_map.163) | data formatting | bytes 1769472 | tf_op jit(solution)/shard_map/pallas_call | solution.py:559
  (2 shorter events, 0.1 us)

commit v4 on v3

--- a/solution.py
+++ b/solution.py
@@ -560,7 +560,7 @@
         kernel,
         out_shape=jax.ShapeDtypeStruct((2, 72, 12, 256), BF),
         in_specs=[hbm, vmem] + [hbm] * 15,
-        out_specs=hbm,
+        out_specs=vmem,
         scratch_shapes=[pltpu.VMEM((2, 4, 4, 4, 32, w), BF) for w in WIDTHS]
         + [
             pltpu.VMEM((2, 42, 24, 512), BF), pltpu.VMEM((36, 16, 512), BF), pltpu.VMEM((36, 16, 512), BF),

time: 129 us -> 130 us (level)
  no operation moved by 1% of the time
where the time goes in v4:
time: 130 us
  Pallas kernels  124 us (95%)
  local copies, waits for them, and re-layouts  5.79 us (4%)
    pallas_call x1, Pallas kernels, body(): pl.pallas_call(kernel, out_shape=jax.ShapeDtypeStruct((2, 72, 12, 256), B...  124 us

profile of v4, /device:TPU:1, one launch (start us, length us, event | category | flops | bytes accessed | tf_op | source)
XLA Modules:
  0.0 130.0 jit_solution(576961485665208775)
XLA Ops:
  0.0 0.8 constant_dynamic-slice_fusion.6
  0.8 1.0 constant_dynamic-slice_fusion.5
  1.9 0.1 constant_dynamic-slice_fusion.3
  2.0 0.1 constant_dynamic-slice_fusion
  2.1 0.1 pad_add_fusion.1
  2.2 0.2 reshape.6
  2.5 0.1 copy.21
  2.6 0.9 reshape.7.ids
  3.5 124.0 %shard_map.163 = bf16[2,72,12,256]{3,2,1,0:T(8,128)(2,1)} custom-call(bf16[2,36,24,512]{3,2,1,0:T(8,128)(2,1)} %latents.1, s32[21,144]{1,0:T(8,128)} %reshape.7.ids, bf16[3,512,512]{2,1,0:T(8,128)(2,1)} %attend_h.1, bf16[512,512]{1,0:T(8,128)(2,1)} %project_h.1, bf16[512,2048]{1,0:T(8,128)(2,1)} %expand_h.1, bf16[2048,512]{1,0:T(8,128)(2,1)} %shrink_h.1, ...), custom_call_target="tpu_custom_call" | custom-call | flops 24000000000 | bytes 10000000 | tf_op jit(solution)/shard_map/pallas_call | solution.py:559
  127.5 2.5 %copy.22 = bf16[2,72,12,256]{3,1,2,0:T(8,128)(2,1)} copy(bf16[2,72,12,256]{3,2,1,0:T(8,128)(2,1)} %shard_map.163) | data formatting | bytes 1769472 | tf_op jit(solution)/shard_map/pallas_call | solution.py:559
  (2 shorter events, 0.1 us)
